TPU v7x, 32 devices: a whole 2x2x4 slice. The times are simulated.
32 devices in a mesh: groups: 2 (over y), leaf: 4 (over z), sample: 4 (over x, core).
Axes of the slice: x: 2, y: 2, z: 4, core: 2. Of those that a mesh axis runs over, the one named last changes fastest.
Arguments:
- points: bfloat16 [16384, 256], P(('groups', 'leaf', 'sample')), parts along dimension 0, may hold values from -40 to 40
- cotangent: bfloat16 [16384, 256], P(('groups', 'leaf', 'sample')), parts along dimension 0, may hold values from -6 to 6
- dest_pos: int32 [16384], P(('groups', 'leaf', 'sample')), parts along dimension 0, may hold values from 0 to 8191, as said below
- w_qkv: bfloat16 [256, 768], replicated, may hold values from -8 to 8
- w_out: bfloat16 [256, 256], replicated, may hold values from -0.375 to 0.375
- w_up: bfloat16 [256, 1024], replicated, may hold values from -0.375 to 0.375
- w_down: bfloat16 [1024, 256], replicated, may hold values from -0.1875 to 0.1875
- gain_attn: float32 [256], replicated, may hold values from 0.1 to 1.9
- gain_mlp: float32 [256], replicated, may hold values from 0.1 to 1.9
Outputs:
- grad_points: bfloat16 [16384, 256], P(('groups', 'leaf', 'sample')), parts along dimension 0
- grad_w_qkv: float32 [512, 768], P(('groups', 'leaf')), parts along dimension 0
- grad_w_out: float32 [512, 256], P(('groups', 'leaf')), parts along dimension 0
- grad_w_up: float32 [512, 1024], P(('groups', 'leaf')), parts along dimension 0
- grad_w_down: float32 [2048, 256], P(('groups', 'leaf')), parts along dimension 0
- grad_gain_attn: float32 [512], P(('groups', 'leaf')), parts along dimension 0
- grad_gain_mlp: float32 [512], P(('groups', 'leaf')), parts along dimension 0
There are 2 independent parts, one for each index of `groups`. A program takes and returns all parts, laid end to end along the dimension named above; an argument that names none is the same for every part. Nothing has to cross between parts.
Inputs may be any that keep to these rules, and one draw needn't show every extreme that they name: `dest_pos`: a permutation of the 8192 positions; of the 512 points of one device, at most 64 have positions in any one aligned block of 512 positions, and in every draw some device reaches exactly 64 for some block.
All inputs are finite; a program needn't handle non-finite values.
Results may differ from a plain program's by a relative error of at most 0.0059.
The roundings to bfloat16 on the way count: a program that leaves them out, or rounds other values in their place, can miss the bound.
Values may be sent and summed in bfloat16 or wider, within the bound.
A program may use at most 64 MiB of HBM per device.

v0:
```python
import math

import jax
import jax.numpy as jnp
from jax import lax
from jax.sharding import PartitionSpec as P

HEADS = 8
BALL = 256
HEAD_DIM = 32


EPSILON = 1e-06
GELU_COEF = math.sqrt(2.0 / math.pi)


def rms_scale(matrix):
    return lax.rsqrt(jnp.mean(matrix * matrix, axis=1, keepdims=True) + EPSILON)


def gelu_parts(pre_act):
    tanh_val = jnp.tanh(GELU_COEF * (pre_act + 0.044715 * pre_act * pre_act * pre_act))
    value = 0.5 * pre_act * (1.0 + tanh_val)
    slope = 0.5 * (1.0 + tanh_val) + 0.5 * pre_act * (1.0 - tanh_val * tanh_val) * GELU_COEF * (
        1.0 + 3.0 * 0.044715 * pre_act * pre_act
    )
    return (value, slope)


def ball_split(ball_block):
    ball_groups = ball_block.shape[0] // BALL
    split_parts = ball_block.reshape(ball_groups, BALL, 3, HEADS, HEAD_DIM)
    return (split_parts[:, :, 0], split_parts[:, :, 1], split_parts[:, :, 2])


def softmax_probs(queries, key_rows):
    scores = jnp.einsum(
        "gqhd,gkhd->ghqk", queries, key_rows, preferred_element_type=jnp.float32
    ) * HEAD_DIM ** (-0.5)
    return jax.nn.softmax(scores, axis=-1)


def ball_forward(operands):
    queries, key_rows, values = ball_split(operands[0])
    probs_low = softmax_probs(queries, key_rows).astype(jnp.bfloat16)
    mixed = jnp.einsum("ghqk,gkhd->gqhd", probs_low, values, preferred_element_type=jnp.float32)
    return mixed.reshape(-1, HEADS * HEAD_DIM).astype(jnp.bfloat16)


def ball_backward(operands):
    ball_block, grad_block = operands
    queries, key_rows, values = ball_split(ball_block)
    attn_probs = softmax_probs(queries, key_rows)
    probs_low = attn_probs.astype(jnp.bfloat16)
    upstream = grad_block.reshape(queries.shape)
    grad_values = jnp.einsum(
        "ghqk,gqhd->gkhd", probs_low, upstream, preferred_element_type=jnp.float32
    )
    grad_probs = jnp.einsum("gqhd,gkhd->ghqk", upstream, values, preferred_element_type=jnp.float32)
    row_delta = jnp.sum(grad_probs * attn_probs, axis=-1, keepdims=True)
    grad_scores = (attn_probs * (grad_probs - row_delta)).astype(jnp.bfloat16)
    grad_queries = jnp.einsum(
        "ghqk,gkhd->gqhd", grad_scores, key_rows, preferred_element_type=jnp.float32
    ) * HEAD_DIM ** (-0.5)
    grad_keys = jnp.einsum(
        "ghqk,gqhd->gkhd", grad_scores, queries, preferred_element_type=jnp.float32
    ) * HEAD_DIM ** (-0.5)
    stacked = jnp.stack([grad_queries, grad_keys, grad_values], axis=2)
    return stacked.reshape(-1, 3 * HEADS * HEAD_DIM).astype(jnp.bfloat16)


def over_balls(function, operands):
    row_count = operands[0].shape[0]
    ball_count = row_count // BALL
    per_group = math.gcd(ball_count, max(1, 512 // BALL))
    shaped = tuple(
        (
            operand.reshape(ball_count // per_group, per_group * BALL, operand.shape[1])
            for operand in operands
        )
    )
    result = lax.map(function, shaped)
    return result.reshape(row_count, result.shape[2])


def layer_grads(rotated, rot_cot, w_qkv, w_out, w_up, w_down, gain_attn, gain_mlp):
    rotated_f = rotated.astype(jnp.float32)
    scale_one = rms_scale(rotated_f)
    norm_one = rotated_f * scale_one
    normed_one = (norm_one * gain_attn).astype(jnp.bfloat16)
    qkv_rows = jnp.dot(normed_one, w_qkv, preferred_element_type=jnp.float32).astype(jnp.bfloat16)
    attended = over_balls(ball_forward, (qkv_rows,))
    middle = rotated_f + jnp.dot(attended, w_out, preferred_element_type=jnp.float32)
    scale_two = rms_scale(middle)
    norm_two = middle * scale_two
    normed_two = (norm_two * gain_mlp).astype(jnp.bfloat16)
    pre_act = jnp.dot(normed_two, w_up, preferred_element_type=jnp.float32)
    act_value, act_slope = gelu_parts(pre_act)
    hidden = act_value.astype(jnp.bfloat16)
    grad_down = jnp.dot(hidden.T, rot_cot, preferred_element_type=jnp.float32)
    grad_pre = (jnp.dot(rot_cot, w_down.T, preferred_element_type=jnp.float32) * act_slope).astype(
        jnp.bfloat16
    )
    grad_up = jnp.dot(normed_two.T, grad_pre, preferred_element_type=jnp.float32)
    grad_normed_two = jnp.dot(grad_pre, w_up.T, preferred_element_type=jnp.float32)
    grad_gain_two = jnp.sum(grad_normed_two * norm_two, axis=0)
    inner_two = grad_normed_two * gain_mlp
    grad_middle = rot_cot.astype(jnp.float32) + scale_two * (
        inner_two - norm_two * jnp.mean(inner_two * norm_two, axis=1, keepdims=True)
    )
    grad_middle_low = grad_middle.astype(jnp.bfloat16)
    grad_out = jnp.dot(attended.T, grad_middle_low, preferred_element_type=jnp.float32)
    grad_attended = jnp.dot(grad_middle_low, w_out.T, preferred_element_type=jnp.float32).astype(
        jnp.bfloat16
    )
    grad_qkv_rows = over_balls(ball_backward, (qkv_rows, grad_attended))
    grad_qkv = jnp.dot(normed_one.T, grad_qkv_rows, preferred_element_type=jnp.float32)
    grad_normed_one = jnp.dot(grad_qkv_rows, w_qkv.T, preferred_element_type=jnp.float32)
    grad_gain_one = jnp.sum(grad_normed_one * norm_one, axis=0)
    inner_one = grad_normed_one * gain_attn
    grad_rot = grad_middle + scale_one * (
        inner_one - norm_one * jnp.mean(inner_one * norm_one, axis=1, keepdims=True)
    )
    return (grad_rot, grad_qkv, grad_out, grad_up, grad_down, grad_gain_one, grad_gain_two)


def local(points, cotangent, dest_pos, w_qkv, w_out, w_up, w_down, gain_attn, gain_mlp):
    row_count, feat_width = points.shape
    peer_count = lax.axis_size(("leaf", "sample"))
    capacity = 2 * row_count // peer_count
    owner_dev = dest_pos // row_count
    target_row = dest_pos % row_count
    one_hot = (owner_dev[:, None] == jnp.arange(peer_count, dtype=jnp.int32)[None, :]).astype(
        jnp.int32
    )
    rank_within = jnp.sum(jnp.cumsum(one_hot, axis=0) * one_hot, axis=1) - 1
    slot_index = owner_dev * capacity + rank_within
    send_points = (
        jnp.zeros((peer_count * capacity, feat_width), jnp.bfloat16).at[slot_index].set(points)
    )
    send_cot = (
        jnp.zeros((peer_count * capacity, feat_width), jnp.bfloat16).at[slot_index].set(cotangent)
    )
    send_target = (
        jnp.full((peer_count * capacity,), row_count, jnp.int32).at[slot_index].set(target_row)
    )
    recv_points, recv_cot, recv_target = (
        lax.all_to_all(
            send_points.reshape(peer_count, capacity, feat_width),
            ("leaf", "sample"),
            split_axis=0,
            concat_axis=0,
            tiled=True,
        ),
        lax.all_to_all(
            send_cot.reshape(peer_count, capacity, feat_width),
            ("leaf", "sample"),
            split_axis=0,
            concat_axis=0,
            tiled=True,
        ),
        lax.all_to_all(
            send_target.reshape(peer_count, capacity),
            ("leaf", "sample"),
            split_axis=0,
            concat_axis=0,
            tiled=True,
        ),
    )
    flat_target = recv_target.reshape(-1)
    rotated = (
        jnp.zeros((row_count, feat_width), jnp.bfloat16)
        .at[flat_target]
        .set(recv_points.reshape(-1, feat_width), mode="drop")
    )
    rot_cot = (
        jnp.zeros((row_count, feat_width), jnp.bfloat16)
        .at[flat_target]
        .set(recv_cot.reshape(-1, feat_width), mode="drop")
    )
    grad_rot, grad_qkv, grad_out, grad_up, grad_down, grad_gain_one, grad_gain_two = layer_grads(
        rotated, rot_cot, w_qkv, w_out, w_up, w_down, gain_attn, gain_mlp
    )
    back_rows = grad_rot.astype(jnp.bfloat16)[jnp.minimum(flat_target, row_count - 1)]
    returned = lax.all_to_all(
        back_rows.reshape(peer_count, capacity, feat_width),
        ("leaf", "sample"),
        split_axis=0,
        concat_axis=0,
        tiled=True,
    )
    grad_points = returned.reshape(-1, feat_width)[slot_index]
    inv_root = 1.0 / math.sqrt(row_count * peer_count)
    shares = (
        lax.psum_scatter(grad_qkv, "leaf", scatter_dimension=0, tiled=True),
        lax.psum_scatter(grad_out, "leaf", scatter_dimension=0, tiled=True),
        lax.psum_scatter(grad_up, "leaf", scatter_dimension=0, tiled=True),
        lax.psum_scatter(grad_down, "leaf", scatter_dimension=0, tiled=True),
        lax.psum_scatter(grad_gain_one, "leaf", scatter_dimension=0, tiled=True),
        lax.psum_scatter(grad_gain_two, "leaf", scatter_dimension=0, tiled=True),
    )
    totals = lax.psum((shares[0], shares[1], shares[2], shares[3], shares[4], shares[5]), "sample")
    return (
        grad_points,
        totals[0] * inv_root,
        totals[1] * inv_root,
        totals[2] * inv_root,
        totals[3] * inv_root,
        totals[4] * inv_root,
        totals[5] * inv_root,
    )


def solution(mesh):
    in_specs = (
        P(("groups", "leaf", "sample"), None),
        P(("groups", "leaf", "sample"), None),
        P(("groups", "leaf", "sample")),
        P(),
        P(),
        P(),
        P(),
        P(),
        P(),
    )
    out_specs = (
        P(("groups", "leaf", "sample"), None),
        P(("groups", "leaf"), None),
        P(("groups", "leaf"), None),
        P(("groups", "leaf"), None),
        P(("groups", "leaf"), None),
        P(("groups", "leaf")),
        P(("groups", "leaf")),
    )
    return jax.shard_map(local, mesh=mesh, in_specs=in_specs, out_specs=out_specs, check_vma=False)
```

profile of v0, /device:TPU:0, one launch (start us, length us, event | category | flops | bytes accessed | tf_op | source)
XLA Modules:
  0.0 249.3 jit_solution(2096667558495499400)
XLA Ops:
  9.5 2.4 scatter_custom_fusion
  12.6 7.4 %all-to-all-start = ((s32[16,1,64]{2,1,0:T(1,128)}), s32[16,1,64]{2,1,0:T(1,128)S(1)}, u32[]{:S(2)}, u32[]{:S(2)}) async-start(s32[16,1,64]{2,1,0:T(1,128)} %all_to_all.15), calls=%async_computation | async-start | bytes 16384 | tf_op jit(solution)/shard_map/all_to_all | solution.py:162
  20.0 3.5 %scatter_custom_fusion.3 = bf16[1024,256]{1,0:T(8,128)(2,1)} fusion(s32[512]{0:T(512)S(1)} %compare_select_fusion.2, bf16[512,256]{1,0:T(8,128)(2,1)} %param.9, bf16[]{:T(256)} %constant.52.clone.1), kind=kCustom, calls=%fused_computation.65 | custom fusion | bytes 524800 | tf_op jit(solution)/shard_map/scatter | solution.py:139
  23.5 2.8 %all-to-all-done = s32[16,1,64]{2,1,0:T(1,128)S(1)} async-done(((s32[16,1,64]{2,1,0:T(1,128)}), s32[16,1,64]{2,1,0:T(1,128)S(1)}, u32[]{:S(2)}, u32[]{:S(2)}) %all-to-all-start) | async-done | bytes 4128 | tf_op jit(solution)/shard_map/all_to_all | solution.py:162
  26.3 3.7 %all-to-all-start.2 = ((bf16[16,64,256]{2,1,0:T(8,128)(2,1)}), bf16[16,64,256]{2,1,0:T(8,128)(2,1)S(1)}, u32[]{:S(2)}, u32[]{:S(2)}) async-start(bf16[16,64,256]{2,1,0:T(8,128)(2,1)} %bitcast.5), calls=%async_computation.2 | async-start | bytes 1048576 | tf_op jit(solution)/shard_map/all_to_all | solution.py:148
  30.0 3.5 %scatter_custom_fusion.1 = bf16[1024,256]{1,0:T(8,128)(2,1)} fusion(s32[512]{0:T(512)S(1)} %compare_select_fusion.2, bf16[512,256]{1,0:T(8,128)(2,1)} %param.10, bf16[]{:T(256)} %constant.52.clone.1), kind=kCustom, calls=%fused_computation.67 | custom fusion | bytes 524800 | tf_op jit(solution)/shard_map/scatter | solution.py:142
  33.5 10.9 %all-to-all-done.2 = bf16[16,64,256]{2,1,0:T(8,128)(2,1)S(1)} async-done(((bf16[16,64,256]{2,1,0:T(8,128)(2,1)}), bf16[16,64,256]{2,1,0:T(8,128)(2,1)S(1)}, u32[]{:S(2)}, u32[]{:S(2)}) %all-to-all-start.2) | async-done | bytes 524320 | tf_op jit(solution)/shard_map/all_to_all | solution.py:148
  44.4 4.0 %all-to-all-start.1 = ((bf16[16,64,256]{2,1,0:T(8,128)(2,1)}), bf16[16,64,256]{2,1,0:T(8,128)(2,1)S(1)}, u32[]{:S(2)}, u32[]{:S(2)}) async-start(bf16[16,64,256]{2,1,0:T(8,128)(2,1)} %bitcast.3), calls=%async_computation.1 | async-start | bytes 1048576 | tf_op jit(solution)/shard_map/all_to_all | solution.py:155
  49.8 5.0 %scatter_custom_fusion.4 = bf16[512,256]{1,0:T(8,128)(2,1)S(1)} fusion(s32[1024]{0:T(1024)S(1)} %bitcast.116, bf16[1024,256]{1,0:T(8,128)(2,1)S(1)} %bitcast.113, bf16[]{:T(256)} %constant.52.clone.1), kind=kCustom, calls=%fused_computation.78 | custom fusion | bytes 262146 | tf_op jit(solution)/shard_map/scatter | solution.py:174
  55.0 7.9 %all-to-all-done.1 = bf16[16,64,256]{2,1,0:T(8,128)(2,1)S(1)} async-done(((bf16[16,64,256]{2,1,0:T(8,128)(2,1)}), bf16[16,64,256]{2,1,0:T(8,128)(2,1)S(1)}, u32[]{:S(2)}, u32[]{:S(2)}) %all-to-all-start.1) | async-done | bytes 524320 | tf_op jit(solution)/shard_map/all_to_all | solution.py:155
  62.9 5.1 %scatter_custom_fusion.2 = bf16[512,256]{1,0:T(8,128)(2,1)S(1)} fusion(s32[1024]{0:T(1024)S(1)} %bitcast.117, bf16[1024,256]{1,0:T(8,128)(2,1)S(1)} %bitcast.112, bf16[]{:T(256)} %constant.52.clone.1), kind=kCustom, calls=%fused_computation.80 | custom fusion | bytes 262146 | tf_op jit(solution)/shard_map/scatter | solution.py:179
  70.1 3.5 %fusion.67 = (f32[2,8,256]{2,1,0:T(8,128)S(1)}, f32[2,8,256,256]{2,3,1,0:T(8,128)}) fusion(bf16[2,256,1,8,32]{1,0,4,3,2:T(2,128)(2,1)S(1)} %get-tuple-element.41, bf16[2,256,1,8,32]{1,0,4,3,2:T(2,128)(2,1)S(1)} %get-tuple-element.40), kind=kOutput, calls=%fused_computation.122 | convolution fusion | flops 70254848 | bytes 4734976 | tf_op jit(solution)/shard_map/while/body/eval_jaxpr/sub | solution.py:40
  74.2 2.6 %fusion.16 = bf16[2,256,8,32]{1,3,2,0:T(8,128)(2,1)S(1)} fusion(bf16[2,256,1,8,32]{1,0,4,3,2:T(2,128)(2,1)S(1)} %get-tuple-element.42, f32[2,8,256,256]{2,3,1,0:T(8,128)} %get-tuple-element.48, f32[2,8,256]{2,1,0:T(8,128)S(1)} %get-tuple-element.47), kind=kOutput, calls=%fused_computation.36 | convolution fusion | flops 69337088 | bytes 4734976 | tf_op jit(solution)/shard_map/while/body/eval_jaxpr/ghqk,gkhd->gqhd/dot_general | solution.py:46
  84.1 3.8 %fusion.17 = bf16[2,256,1,8,32]{1,4,3,0,2:T(8,128)(2,1)} fusion(bf16[2,256,8,32]{1,0,3,2:T(2,128)(2,1)S(1)} %reshape.169, f32[2,8,256,256]{2,3,1,0:T(8,128)} %get-tuple-element.48, f32[2,8,256]{2,1,0:T(8,128)} %copy-done.15), kind=kOutput, calls=%fused_computation.37 | convolution fusion | flops 69337088 | bytes 4734976 | tf_op jit(solution)/shard_map/while/body/eval_jaxpr/ghqk,gqhd->gkhd/dot_general | solution.py:56
  87.9 2.8 %multiply_reduce_fusion = (f32[2,8,256]{2,1,0:T(8,128)S(1)}, f32[2,8,256,256]{2,3,1,0:T(8,128)}) fusion(f32[2,8,256,256]{2,3,1,0:T(8,128)S(1)} %copy-done.1, f32[2,8,256]{2,1,0:T(8,128)S(1)} %copy-done.16, bf16[2,256,1,8,32]{1,0,4,3,2:T(2,128)(2,1)S(1)} %copy-done.12, bf16[2,256,8,32]{1,0,3,2:T(2,128)(2,1)S(1)} %reshape.169), kind=kOutput, calls=%fused_computation.9 | convolution fusion | flops 70250496 | bytes 8945664 | tf_op jit(solution)/shard_map/while/body/eval_jaxpr/gqhd,gkhd->ghqk/dot_general | solution.py:59
  90.8 4.3 %multiply_convert_fusion = bf16[2,8,256,256]{2,3,1,0:T(8,128)(2,1)S(1)} fusion(f32[2,8,256,256]{2,3,1,0:T(8,128)} %get-tuple-element.53, f32[2,8,256]{2,1,0:T(8,128)S(1)} %get-tuple-element.52, f32[2,8,256,256]{2,3,1,0:T(8,128)} %get-tuple-element.48, f32[2,8,256]{2,1,0:T(8,128)S(1)} %copy-done.16), kind=kLoop, calls=%fused_computation.8 | loop fusion | flops 4194304 | bytes 10518528 | tf_op jit(solution)/shard_map/while/body/eval_jaxpr/convert_element_type | solution.py:61
  100.1 3.4 %fusion.20 = f32[1024,256]{1,0:T(8,128)} fusion(bf16[512,256]{1,0:T(8,128)(2,1)S(1)} %scatter_custom_fusion.2, f32[512,1024]{1,0:T(8,128)} %copy-done.3), kind=kOutput, calls=%fused_computation.40 | convolution fusion | flops 273154048 | bytes 3407872 | tf_op jit(solution)/shard_map/dot_general | solution.py:100
  103.6 1.5 fusion.64
  105.2 1.6 fusion.31
  107.2 4.9 %gather_fusion = bf16[1024,256]{1,0:T(8,128)(2,1)} fusion(bf16[512,256]{1,0:T(8,128)(2,1)S(1)} %copy.69, s32[1024]{0:T(1024)S(1)} %broadcast_clamp_fusion), kind=kCustom, calls=%fused_computation | custom fusion | bytes 1052672 | tf_op jit(solution)/shard_map/gather | solution.py:184
  112.1 4.1 %all-to-all-start.3 = ((bf16[16,64,256]{2,1,0:T(8,128)(2,1)}), bf16[16,64,256]{2,1,0:T(8,128)(2,1)S(1)}, u32[]{:S(2)}, u32[]{:S(2)}) async-start(bf16[16,64,256]{2,1,0:T(8,128)(2,1)} %bitcast.18), calls=%async_computation.3 | async-start | bytes 1048576 | tf_op jit(solution)/shard_map/all_to_all | solution.py:185
  116.3 25.9 %reduce-scatter.5.cloned.1.call-done = f32[64,768]{1,0:T(8,128)} async-done(((f32[256,768]{1,0:T(8,128)}), f32[64,768]{1,0:T(8,128)}) %reduce-scatter.5.cloned.1.call-update) | async-done | bytes 196624 | tf_op jit(solution)/shard_map/reduce_scatter | solution.py:195
  142.2 29.9 %reduce-scatter.11.cloned.1.call-done = f32[256,256]{1,0:T(8,128)} async-done(((f32[1024,256]{1,0:T(8,128)}), f32[256,256]{1,0:T(8,128)}) %reduce-scatter.11.cloned.1.call-update) | async-done | bytes 262160 | tf_op jit(solution)/shard_map/reduce_scatter | solution.py:198
  172.1 28.0 %reduce-scatter.9.cloned.1.call-done = f32[64,1024]{1,0:T(8,128)} async-done(((f32[256,1024]{1,0:T(8,128)}), f32[64,1024]{1,0:T(8,128)}) %reduce-scatter.9.cloned.1.call-update) | async-done | bytes 262160 | tf_op jit(solution)/shard_map/reduce_scatter | solution.py:197
  201.3 9.4 %all-reduce.4 = (f32[256]{0:T(256)S(1)}, f32[256]{0:T(256)S(1)}) all-reduce(f32[256]{0:T(256)S(1)} %get-tuple-element.30, f32[256]{0:T(256)S(1)} %copy-done.21), channel_id=6, replica_groups=mesh['groups'=2,'leaf'=4,'sample'=4] {'leaf'}, use_global_device_ids=true, to_apply=%region_24.25.clone | all-reduce | flops 512 | bytes 4096
  210.9 6.0 %all-reduce.2 = (f32[64]{0:T(128)S(1)}, f32[64]{0:T(128)S(1)}) all-reduce(f32[64]{0:T(128)S(1)} %dynamic-slice.3, f32[64]{0:T(128)S(1)} %dynamic-slice.5), channel_id=1, replica_groups=mesh['groups'=2,'leaf'=4,'sample'=4] {'sample'}, use_global_device_ids=true, to_apply=%region_25.26 | all-reduce | flops 128 | bytes 1024 | tf_op jit(solution)/shard_map/psum | solution.py:202
  217.4 2.6 %gather_fusion.1 = bf16[512,256]{1,0:T(8,128)(2,1)} fusion(bf16[1024,256]{1,0:T(8,128)(2,1)S(1)} %bitcast.105, s32[1024]{0:T(1024)S(1)} %pad_clamp_fusion), kind=kCustom, calls=%fused_computation.1 | custom fusion | bytes 526336 | tf_op jit(solution)/shard_map/gather | solution.py:192
  220.0 16.4 %all-reduce.7.cloned.1.call-done = (f32[64,768]{1,0:T(8,128)}, f32[64,256]{1,0:T(8,128)}, f32[64,1024]{1,0:T(8,128)}, f32[256,256]{1,0:T(8,128)}) async-done(((f32[64,768]{1,0:T(8,128)}, f32[64,256]{1,0:T(8,128)}, f32[64,1024]{1,0:T(8,128)}, f32[256,256]{1,0:T(8,128)}), (f32[64,768]{1,0:T(8,128)}, f32[64,256]{1,0:T(8,128)}, f32[64,1024]{1,0:T(8,128)}, f32[256,256]{1,0:T(8,128)})) %all-reduce.7.cloned.1.call-update) | async-done | bytes 786448 | tf_op jit(solution)/shard_map/psum | solution.py:202
  236.4 1.6 broadcast_multiply_fusion.2
  238.0 1.5 broadcast_multiply_fusion.3
  239.5 1.7 broadcast_multiply_fusion.1
  241.1 1.7 broadcast_multiply_fusion
  (109 shorter events, 20.9 us)
Async XLA Ops:
  7.2 70.3 %copy-start = (bf16[256,1024]{1,0:T(8,128)(2,1)S(1)}, bf16[256,1024]{1,0:T(8,128)(2,1)}, u32[]{:S(2)}) copy-start(bf16[256,1024]{1,0:T(8,128)(2,1)} %param.14) | copy-start | bytes 1572868
  9.5 39.1 %copy-start.19 = (s32[512]{0:T(512)}, s32[512]{0:T(512)S(1)}, u32[]{:S(2)}) copy-start(s32[512]{0:T(512)S(1)} %compare_select_fusion.2) | copy-start | bytes 6148
  12.6 13.7 %all-to-all-start = ((s32[16,1,64]{2,1,0:T(1,128)}), s32[16,1,64]{2,1,0:T(1,128)S(1)}, u32[]{:S(2)}, u32[]{:S(2)}) async-start(s32[16,1,64]{2,1,0:T(1,128)} %all_to_all.15), calls=%async_computation | async-start | bytes 16384 | tf_op jit(solution)/shard_map/all_to_all | solution.py:162
  26.3 41.9 %copy-start.9 = (bf16[256,768]{1,0:T(8,128)(2,1)S(1)}, bf16[256,768]{1,0:T(8,128)(2,1)}, u32[]{:S(2)}) copy-start(bf16[256,768]{1,0:T(8,128)(2,1)} %param.12) | copy-start | bytes 1179652
  26.3 41.9 %copy-start.17 = (f32[256]{0:T(256)S(1)}, f32[256]{0:T(256)}, u32[]{:S(2)}) copy-start(f32[256]{0:T(256)} %param.16) | copy-start | bytes 3076
  26.3 18.1 %all-to-all-start.2 = ((bf16[16,64,256]{2,1,0:T(8,128)(2,1)}), bf16[16,64,256]{2,1,0:T(8,128)(2,1)S(1)}, u32[]{:S(2)}, u32[]{:S(2)}) async-start(bf16[16,64,256]{2,1,0:T(8,128)(2,1)} %bitcast.5), calls=%async_computation.2 | async-start | bytes 1048576 | tf_op jit(solution)/shard_map/all_to_all | solution.py:148
  44.4 18.5 %all-to-all-start.1 = ((bf16[16,64,256]{2,1,0:T(8,128)(2,1)}), bf16[16,64,256]{2,1,0:T(8,128)(2,1)S(1)}, u32[]{:S(2)}, u32[]{:S(2)}) async-start(bf16[16,64,256]{2,1,0:T(8,128)(2,1)} %bitcast.3), calls=%async_computation.1 | async-start | bytes 1048576 | tf_op jit(solution)/shard_map/all_to_all | solution.py:155
  48.5 67.8 %reduce-scatter.7.cloned.1.call-start = ((), (), s32[]{:S(2)}) async-start(), calls=%async_computation.9 | async-start | bytes 327680 | tf_op jit(solution)/shard_map/reduce_scatter | solution.py:196
  70.0 3.5 %copy-start.4 = (bf16[2,256,1,8,32]{1,0,4,3,2:T(2,128)(2,1)}, bf16[2,256,1,8,32]{1,0,4,3,2:T(2,128)(2,1)S(1)}, u32[]{:S(2)}) copy-start(bf16[2,256,1,8,32]{1,0,4,3,2:T(2,128)(2,1)S(1)} %get-tuple-element.40) | copy-start | bytes 786436
  70.0 3.5 %copy-start.6 = (bf16[2,256,1,8,32]{1,0,4,3,2:T(2,128)(2,1)}, bf16[2,256,1,8,32]{1,0,4,3,2:T(2,128)(2,1)S(1)}, u32[]{:S(2)}) copy-start(bf16[2,256,1,8,32]{1,0,4,3,2:T(2,128)(2,1)S(1)} %get-tuple-element.41) | copy-start | bytes 786436
  70.1 3.5 %copy-start.11 = (bf16[2,256,1,8,32]{1,0,4,3,2:T(2,128)(2,1)}, bf16[2,256,1,8,32]{1,0,4,3,2:T(2,128)(2,1)S(1)}, u32[]{:S(2)}) copy-start(bf16[2,256,1,8,32]{1,0,4,3,2:T(2,128)(2,1)S(1)} %get-tuple-element.42) | copy-start | bytes 786436
  74.2 3.0 %copy-start.8 = (bf16[256,256]{1,0:T(8,128)(2,1)S(1)}, bf16[256,256]{1,0:T(8,128)(2,1)}, u32[]{:S(2)}) copy-start(bf16[256,256]{1,0:T(8,128)(2,1)} %param.13) | copy-start | bytes 393220
  76.8 0.7 copy-start.14
  77.1 1.0 copy-start.22
  78.2 1.5 copy-start.3
  84.1 3.8 %copy-start.1 = (f32[2,8,256,256]{2,3,1,0:T(8,128)S(1)}, f32[2,8,256,256]{2,3,1,0:T(8,128)}, u32[]{:S(2)}) copy-start(f32[2,8,256,256]{2,3,1,0:T(8,128)} %get-tuple-element.48) | copy-start | bytes 12582916
  84.1 3.8 %copy-start.12 = (bf16[2,256,1,8,32]{1,0,4,3,2:T(2,128)(2,1)S(1)}, bf16[2,256,1,8,32]{1,0,4,3,2:T(2,128)(2,1)}, u32[]{:S(2)}) copy-start(bf16[2,256,1,8,32]{1,0,4,3,2:T(2,128)(2,1)} %copy-done.11) | copy-start | bytes 786436
  84.1 3.8 %copy-start.16 = (f32[2,8,256]{2,1,0:T(8,128)S(1)}, f32[2,8,256]{2,1,0:T(8,128)}, u32[]{:S(2)}) copy-start(f32[2,8,256]{2,1,0:T(8,128)} %copy-done.15) | copy-start | bytes 49156
  90.7 51.5 %reduce-scatter.5.cloned.1.call-start = ((), (), s32[]{:S(2)}) async-start(), calls=%async_computation.8 | async-start | bytes 983040 | tf_op jit(solution)/shard_map/reduce_scatter | solution.py:195
  90.8 4.3 %copy-start.7 = (bf16[2,256,1,8,32]{1,0,4,3,2:T(2,128)(2,1)S(1)}, bf16[2,256,1,8,32]{1,0,4,3,2:T(2,128)(2,1)}, u32[]{:S(2)}) copy-start(bf16[2,256,1,8,32]{1,0,4,3,2:T(2,128)(2,1)} %copy-done.6) | copy-start | bytes 786436
  95.1 1.0 copy-start.5
  95.1 1.4 copy-start.13
  96.5 2.0 copy-start.18
  97.6 0.9 copy-start.2
  99.8 72.2 %reduce-scatter.11.cloned.1.call-start = ((), (), s32[]{:S(2)}) async-start(), calls=%async_computation.11 | async-start | bytes 1310720 | tf_op jit(solution)/shard_map/reduce_scatter | solution.py:198
  103.6 1.6 copy-start.10
  103.6 96.4 %reduce-scatter.9.cloned.1.call-start = ((), (), s32[]{:S(2)}) async-start(), calls=%async_computation.10 | async-start | bytes 1310720 | tf_op jit(solution)/shard_map/reduce_scatter | solution.py:197
  107.1 92.9 %copy-start.23 = (u32[32]{0:T(128)S(1)}, u32[32]{0:T(128)}, u32[]{:S(2)}) copy-start(u32[32]{0:T(128)} %constant.110) | copy-start | bytes 388
  107.1 94.2 %copy-start.20 = (s32[512]{0:T(512)S(1)}, s32[512]{0:T(512)}, u32[]{:S(2)}) copy-start(s32[512]{0:T(512)} %copy-done.19) | copy-start | bytes 6148
  107.1 94.2 %copy-start.21 = (f32[256]{0:T(256)S(1)}, f32[256]{0:T(256)}, u32[]{:S(2)}) copy-start(f32[256]{0:T(256)} %get-tuple-element.28) | copy-start | bytes 3076
  112.1 105.3 %all-to-all-start.3 = ((bf16[16,64,256]{2,1,0:T(8,128)(2,1)}), bf16[16,64,256]{2,1,0:T(8,128)(2,1)S(1)}, u32[]{:S(2)}, u32[]{:S(2)}) async-start(bf16[16,64,256]{2,1,0:T(8,128)(2,1)} %bitcast.18), calls=%async_computation.3 | async-start | bytes 1048576 | tf_op jit(solution)/shard_map/all_to_all | solution.py:185
  116.2 120.2 %all-reduce.7.cloned.1.call-start = ((), (), s32[]{:S(2)}) async-start(), calls=%async_computation.12 | async-start | bytes 1572864 | tf_op jit(solution)/shard_map/psum | solution.py:202
  (1 other events, 0.6 us)
Sparse Core Ops, SparseCore 0:
  90.8 19.1 reduce-scatter.6
  112.4 29.7 reduce-scatter.4
  144.6 27.4 reduce-scatter.10
  174.2 25.7 reduce-scatter.8
  202.6 33.6 all-reduce.6
where the time goes:
time: 250 us; the launch traced here: 249 us
  waiting for transfers between devices  122 us (49%)
  local copies, waits for them, and re-layouts  36.2 us (14%)
  matrix products  26.9 us (11%)
  starting transfers between devices  19.6 us (8%)
  blocking collectives  15.4 us (6%)
  between operations  15 us (6%)
  other arithmetic  14.5 us (6%)
    reduce_scatter x1, waiting for transfers between devices, local(): lax.psum_scatter(grad_down, 'leaf', scatter_dimension=0, tiled=True)  29.9 us
    reduce_scatter x1, waiting for transfers between devices, local(): lax.psum_scatter(grad_up, 'leaf', scatter_dimension=0, tiled=True)  28 us
    reduce_scatter x1, waiting for transfers between devices, local(): lax.psum_scatter(grad_qkv, 'leaf', scatter_dimension=0, tiled=True)  25.9 us
    psum x1, waiting for transfers between devices, local(): lax.psum((shares[0], shares[1], shares[2], shares[3], shares[4], shares[5...  16.4 us
    all_to_all x1, waiting for transfers between devices, local(): lax.all_to_all(send_points.reshape(peer_count, capacity, feat_width), ('l...  10.9 us
    unnamed x1, blocking collectives  9.39 us
    all_to_all x1, waiting for transfers between devices, local(): lax.all_to_all(send_cot.reshape(peer_count, capacity, feat_width), ('leaf...  7.91 us
    all_to_all x1, starting transfers between devices, local(): lax.all_to_all(send_target.reshape(peer_count, capacity), ('leaf', 'sampl...  7.36 us
  transfers between devices with their start and end apart: 9, of which 7 were waited for; matrix products, arithmetic and copies ran while one was open for 15% of the time, Pallas kernels for 0%

commit v1 on v0

v1 whole, which is shorter than its diff:
```python
import math

import jax
import jax.numpy as jnp
from jax import lax
from jax.experimental import pallas as pl
from jax.experimental.pallas import tpu as pltpu
from jax.sharding import PartitionSpec as P

HEADS = 8
BALL = 256
HEAD_DIM = 32
EPSILON = 1e-06
GELU_COEF = math.sqrt(2.0 / math.pi)
LANES = 256
MESH = pl.DeviceIdType.MESH
F32 = jnp.float32
BF16 = jnp.bfloat16


class Sizes:
    def __init__(self, mesh, rows, feat, hid):
        self.leaf = mesh.shape["leaf"]
        self.sample = mesh.shape["sample"]
        self.peers = self.leaf * self.sample
        self.rows = rows
        self.feat = feat
        self.hid = hid
        self.cap = max(16, 2 * rows // self.peers)
        self.slots = self.peers * self.cap
        self.groups = self.slots // LANES
        self.block = feat // self.leaf
        self.wire = BF16 if self.block % 16 == 0 else F32
        self.down = hid // self.peers
        self.inv_root = 1.0 / math.sqrt(rows * self.peers)


def dot(a, b):
    return jnp.dot(a, b, preferred_element_type=F32)


def dot_nt(a, b):
    return lax.dot_general(a, b, (((1,), (1,)), ((), ())), preferred_element_type=F32)


def dot_tn(a, b):
    return lax.dot_general(a, b, (((0,), (0,)), ((), ())), preferred_element_type=F32)


def iota(shape, dim):
    return lax.broadcasted_iota(jnp.int32, shape, dim)


def to_bf(mask):
    return jnp.where(mask, 1.0, 0.0).astype(BF16)


def position(z):
    return lax.axis_index("leaf") * z.sample + lax.axis_index("sample")


def peer_id(z, p):
    return {"leaf": p // z.sample, "sample": p % z.sample}


def greet_all(z):
    me = position(z)
    barrier = pltpu.get_barrier_semaphore()

    def body(d, carry):
        pl.semaphore_signal(
            barrier, inc=1, device_id=peer_id(z, (me + d) % z.peers), device_id_type=MESH
        )
        return carry

    lax.fori_loop(1, z.peers, body, 0)
    pl.semaphore_wait(barrier, z.peers - 1)


def view(z, ref, p, count):
    if count is None:
        return ref.at[p]
    return ref.at[pl.ds(pl.multiple_of(p * count, count), count)]


def swap_copy(z, src, dst, sems, d, there, here, to, count):
    return pltpu.make_async_remote_copy(
        src_ref=view(z, src, there, count),
        dst_ref=view(z, dst, here, count),
        send_sem=sems[0].at[d],
        recv_sem=sems[1].at[here],
        device_id=peer_id(z, to),
        device_id_type=MESH,
    )


def swap_start(z, src, dst, sems, count):
    me = position(z)

    def body(d, carry):
        p = (me + d) % z.peers
        swap_copy(z, src, dst, sems, d, p, me, p, count).start()
        return carry

    near = z.sample
    lax.fori_loop(near, z.peers, body, 0)
    lax.fori_loop(1, near, body, 0)


def swap_recv(z, src, dst, sems, count):
    me = position(z)

    def body(d, carry):
        q = (me + d) % z.peers
        swap_copy(z, src, dst, sems, d, q, q, q, count).wait_recv()
        return carry

    lax.fori_loop(1, z.peers, body, 0)


def swap_sent(z, src, dst, sems, count):
    me = position(z)

    def body(d, carry):
        q = (me + d) % z.peers
        swap_copy(z, src, dst, sems, d, q, q, q, count).wait_send()
        return carry

    lax.fori_loop(1, z.peers, body, 0)


def keep_own(z, src, dst, count):
    me = position(z)
    where = pl.ds(pl.multiple_of(me * count, count), count)
    dst[where, :] = src[where, :]


def split_pos(z, pos):
    bits = z.rows.bit_length() - 1
    return lax.shift_right_logical(pos, bits), jnp.bitwise_and(pos, z.rows - 1)


def prepare(z, drow, tsend, place):
    me = position(z)
    owner, target = split_pos(z, drow[...])
    mine = iota((z.peers, z.rows), 0) == owner
    before = to_bf(iota((z.rows, z.rows), 0) < iota((z.rows, z.rows), 1))
    counts = dot(to_bf(mine), before)
    rank = jnp.sum(jnp.where(mine, counts, 0.0), axis=0, keepdims=True).astype(jnp.int32)
    place[...] = to_bf(iota((z.slots, z.rows), 0) == owner * z.cap + rank)
    shift = (me % (LANES // z.cap)) * z.cap
    at_lane = to_bf(iota((LANES, z.rows), 0) == rank + shift)
    code = target + 1
    high = lax.shift_right_logical(code, 4).astype(F32)
    low = jnp.bitwise_and(code, 15).astype(F32)
    targets = 16.0 * dot_nt(jnp.where(mine, high, 0.0).astype(BF16), at_lane) + dot_nt(
        jnp.where(mine, low, 0.0).astype(BF16), at_lane
    )
    for p in range(z.peers):
        tsend[p] = targets[p : p + 1, :]


def group_targets(z, trecv, g):
    per = LANES // z.cap
    row = trecv[g * per]
    for j in range(1, per):
        row = row + trecv[g * per + j]
    return row


def dispatch_kernel(z, drow, pts, cot, rot, rcot, trecv, place, tsend, psend, csend, precv, crecv, *sems):
    tsems, psems, csems = sems[0:2], sems[2:4], sems[4:6]
    me = position(z)
    greet_all(z)
    prepare(z, drow, tsend, place)
    trecv[me] = tsend[me]
    swap_start(z, tsend, trecv, tsems, None)
    psend[...] = dot(place[...], pts[...]).astype(BF16)
    swap_start(z, psend, precv, psems, z.cap)
    csend[...] = dot(place[...], cot[...]).astype(BF16)
    swap_start(z, csend, crecv, csems, z.cap)
    keep_own(z, psend, precv, z.cap)
    keep_own(z, csend, crecv, z.cap)
    swap_recv(z, tsend, trecv, tsems, None)
    swap_recv(z, psend, precv, psems, z.cap)

    def gather(recv):
        total = None
        for g in range(z.groups):
            pick = to_bf(
                (iota((z.rows, LANES), 0) + 1).astype(F32) == group_targets(z, trecv, g)
            )
            part = dot(pick, recv[g * LANES : (g + 1) * LANES, :])
            total = part if total is None else total + part
        return total.astype(BF16)

    rot[...] = gather(precv)
    swap_recv(z, csend, crecv, csems, z.cap)
    rcot[...] = gather(crecv)
    swap_sent(z, tsend, trecv, tsems, None)
    swap_sent(z, psend, precv, psems, z.cap)
    swap_sent(z, csend, crecv, csems, z.cap)


def scale_of(matrix):
    return lax.rsqrt(jnp.mean(matrix * matrix, axis=1, keepdims=True) + EPSILON)


def head_mask(feat, h, dim):
    shape = (1, feat) if dim == 1 else (feat, 1)
    return lax.shift_right_logical(iota(shape, dim), 5) == h


def attention_forward(z, qkv, probs, att):
    feat = z.feat
    balls = z.rows // BALL
    root = HEAD_DIM**-0.5

    def body(h, totals):
        mask = head_mask(feat, h, 1)
        out = []
        for b in range(balls):
            rows = slice(b * BALL, (b + 1) * BALL)
            zero = jnp.zeros((), BF16)
            q = jnp.where(mask, qkv[rows, 0:feat], zero)
            v = jnp.where(mask, qkv[rows, 2 * feat : 3 * feat], zero)
            scores = dot_nt(q, qkv[rows, feat : 2 * feat]) * root
            e = jnp.exp(scores - jnp.max(scores, axis=1, keepdims=True))
            p = e * (1.0 / jnp.sum(e, axis=1, keepdims=True))
            probs[h * balls + b] = p
            out.append(totals[b] + dot(p.astype(BF16), v))
        return tuple(out)

    start = tuple(jnp.zeros((BALL, feat), F32) for _ in range(balls))
    totals = lax.fori_loop(0, HEADS, body, start)
    for b in range(balls):
        att[b * BALL : (b + 1) * BALL, :] = totals[b].astype(BF16)


def mlp(z, rc, normed_two, w_up, w_down, up, down):
    rows, feat = z.rows, z.feat
    total = None
    n2t = normed_two.T
    width = z.hid // z.sample
    per_leaf = z.hid // z.leaf
    for c in range(z.sample):
        cols = slice(c * width, (c + 1) * width)
        x = dot(normed_two, w_up[:, cols])
        x2 = x * x
        t = jnp.tanh(GELU_COEF * (x + 0.044715 * x2 * x))
        half = 0.5 * (1.0 + t)
        hidden = (x * half).astype(BF16)
        slope = half + 0.5 * x * (1.0 - t * t) * GELU_COEF * (1.0 + 3.0 * 0.044715 * x2)
        gpre = (dot_nt(rc, w_down[cols, :]) * slope).astype(BF16)
        up[c] = dot(n2t, gpre).astype(up.dtype)
        gdown = dot_tn(hidden, rc).astype(down.dtype)
        for r in range(0, width, z.down):
            row = c * width + r
            leaf, inner = row // per_leaf, row % per_leaf
            s = inner // z.down
            down[s, leaf * z.down : (leaf + 1) * z.down, :] = gdown[r : r + z.down, :]
        part = dot_nt(gpre, w_up[:, cols])
        total = part if total is None else total + part
    return total


def attention_backward(z, qkv, probs, gatt, gqt, gkt, gvt, lo, hi, totals):
    feat = z.feat
    balls = z.rows // BALL
    qt, gt, dkt, dvt = gqt

    def body(h, totals):
        mask = head_mask(feat, h, 1)
        head_rows = pl.ds(pl.multiple_of(h * HEAD_DIM, HEAD_DIM), HEAD_DIM)
        out = []
        for b in range(balls):
            rows = slice(b * BALL, (b + 1) * BALL)
            zero = jnp.zeros((), BF16)
            g = jnp.where(mask, gatt[rows, :], zero)
            k = jnp.where(mask, qkv[rows, feat : 2 * feat], zero)
            p = probs[h * balls + b]
            gp = dot_nt(g, qkv[rows, 2 * feat : 3 * feat])
            delta = jnp.sum(gp * p, axis=1, keepdims=True)
            gs = (p * (gp - delta)).astype(BF16)
            out.append(totals[b] + dot(gs, k))
            dkt[b, head_rows, :] = dot(qt[b, head_rows, :], gs)
            dvt[b, head_rows, :] = dot(gt[b, head_rows, :], p.astype(BF16))
        return tuple(out)

    return lax.fori_loop(lo, hi, body, totals)


def layer_kernel(
    z, rot, rcot, w_qkv, w_out, w_up, w_down, gain_attn, gain_mlp,
    grot, up, down, qo, gains,
    qkv, probs, att, gatt, gqkv, qt, gt, dkt, dvt,
):
    feat = z.feat
    balls = z.rows // BALL
    root = HEAD_DIM**-0.5
    rotated = rot[...].astype(F32)
    scale_one = scale_of(rotated)
    norm_one = rotated * scale_one
    normed_one = (norm_one * gain_attn[...]).astype(BF16)
    qkv[...] = dot(normed_one, w_qkv[...]).astype(BF16)
    attention_forward(z, qkv, probs, att)
    middle = rotated + dot(att[...], w_out[...])
    scale_two = scale_of(middle)
    norm_two = middle * scale_two
    normed_two = (norm_two * gain_mlp[...]).astype(BF16)
    rc = rcot[...]
    gn2 = mlp(z, rc, normed_two, w_up, w_down, up, down)
    gains[1:2, :] = jnp.sum(gn2 * norm_two, axis=0, keepdims=True)
    inner_two = gn2 * gain_mlp[...]
    gmid = rc.astype(F32) + scale_two * (
        inner_two - norm_two * jnp.mean(inner_two * norm_two, axis=1, keepdims=True)
    )
    gmid_low = gmid.astype(BF16)
    qo[3] = dot_tn(att[...], gmid_low).astype(qo.dtype)
    gatt[...] = dot_nt(gmid_low, w_out[...]).astype(BF16)
    for b in range(balls):
        rows = slice(b * BALL, (b + 1) * BALL)
        qt[b] = qkv[rows, 0:feat].T
        gt[b] = gatt[rows, :].T
    totals = tuple(jnp.zeros((BALL, feat), F32) for _ in range(balls))
    totals = attention_backward(z, qkv, probs, gatt, (qt, gt, dkt, dvt), None, None, 0, HEADS, totals)
    for b in range(balls):
        rows = slice(b * BALL, (b + 1) * BALL)
        gqkv[rows, 0:feat] = (totals[b] * root).astype(BF16)
        gqkv[rows, feat : 2 * feat] = (dkt[b] * root).astype(BF16).T
        gqkv[rows, 2 * feat : 3 * feat] = dvt[b].astype(BF16).T
    gn1 = dot_nt(gqkv[...], w_qkv[...])
    gains[0:1, :] = jnp.sum(gn1 * norm_one, axis=0, keepdims=True)
    inner_one = gn1 * gain_attn[...]
    grot[...] = (
        gmid
        + scale_one * (inner_one - norm_one * jnp.mean(inner_one * norm_one, axis=1, keepdims=True))
    ).astype(BF16)
    n1t = normed_one.T
    for c in range(3):
        qo[c] = dot(n1t, gqkv[:, c * feat : (c + 1) * feat]).astype(qo.dtype)


class Family:
    def __init__(self, z, own, refs, sems):
        self.z, self.own = z, own
        self.first, self.far, self.second, self.out3, self.third, self.out4, self.fourth = refs
        self.sems = sems
        self.s = lax.axis_index("sample")
        self.l = lax.axis_index("leaf")
        self.pair = self.s + 1 - 2 * (self.s % 2)
        self.cross = (self.s + 2) % 4

    def copy(self, src, dst, i, j, device):
        return pltpu.make_async_remote_copy(
            src_ref=src,
            dst_ref=dst,
            send_sem=self.sems[0].at[i],
            recv_sem=self.sems[1].at[j],
            device_id=device,
            device_id_type=MESH,
        )

    def step1(self):
        pair = {"sample": self.pair}
        return [
            self.copy(self.own.at[(self.pair + 2) % 4], self.first.at[1], 1, 1, pair),
            self.copy(self.own.at[self.pair], self.first.at[0], 0, 0, pair),
        ]

    def start1(self):
        for c in self.step1():
            c.start()

    def step2(self):
        return self.copy(self.far, self.second, 2, 2, {"sample": self.cross})

    def start2(self):
        far, near = self.step1()
        far.wait_recv()
        total = self.own[self.cross].astype(F32) + self.first[1].astype(F32)
        self.far[...] = total.astype(self.far.dtype)
        self.step2().start()
        near.wait_recv()

    def step3(self, d):
        z = self.z
        there = (self.l + d) % z.leaf
        rows = pl.ds(pl.multiple_of(there * z.block, z.block), z.block)
        return (
            self.copy(
                self.out3.at[rows], self.third.at[self.l], 3 + d, 3 + self.l, {"leaf": there}
            ),
            self.copy(
                self.out3.at[rows], self.third.at[there], 3 + d, 3 + there, {"leaf": there}
            ),
        )

    def start3(self):
        self.step2().wait_recv()
        total = (
            self.own[self.s].astype(F32) + self.first[0].astype(F32) + self.second[...].astype(F32)
        )
        self.out3[...] = total.astype(self.out3.dtype)

        def body(d, carry):
            self.step3(d)[0].start()
            return carry

        lax.fori_loop(1, self.z.leaf, body, 0)

    def step4(self, d):
        z = self.z
        there = (self.s + d) % z.sample
        base = 3 + z.leaf
        return (
            self.copy(self.out4, self.fourth.at[self.s], base + d, base + self.s, {"sample": there}),
            self.copy(self.out4, self.fourth.at[there], base + d, base + there, {"sample": there}),
        )

    def start4(self):
        z = self.z

        def body(d, carry):
            self.step3(d)[1].wait_recv()
            return carry

        lax.fori_loop(1, z.leaf, body, 0)
        rows = pl.ds(pl.multiple_of(self.l * z.block, z.block), z.block)
        self.third[self.l] = self.out3[rows, :]
        total = self.third[0].astype(F32)
        for j in range(1, z.leaf):
            total = total + self.third[j].astype(F32)
        self.out4[...] = total.astype(self.out4.dtype)
        self.fourth[self.s] = self.out4[...]
        for d in range(1, z.sample):
            self.step4(d)[0].start()

    def finish(self):
        for d in range(1, self.z.sample):
            self.step4(d)[1].wait_recv()

    def sent(self):
        for c in self.step1():
            c.wait_send()
        self.step2().wait_send()

        def body(d, carry):
            self.step3(d)[0].wait_send()
            return carry

        lax.fori_loop(1, self.z.leaf, body, 0)
        for d in range(1, self.z.sample):
            self.step4(d)[0].wait_send()


def family_scratch(z):
    f, w = z.feat, z.wire
    return [
        pltpu.VMEM((2, f, f), w),
        pltpu.VMEM((f, f), w),
        pltpu.VMEM((f, f), w),
        pltpu.VMEM((f, f), w),
        pltpu.VMEM((z.leaf, z.block, f), w),
        pltpu.VMEM((z.block, f), w),
        pltpu.VMEM((z.sample, z.block, f), w),
    ]


def family_sems(z):
    count = 3 + z.leaf + z.sample
    return [pltpu.SemaphoreType.DMA((count,)), pltpu.SemaphoreType.DMA((count,))]


def back_rows(z, trecv, grot, bsend):
    for g in range(z.groups):
        row = group_targets(z, trecv, g)
        col = jnp.broadcast_to(row, (128, LANES)).T[:, 0:1]
        pick = to_bf((iota((LANES, z.rows), 1) + 1).astype(F32) == col)
        bsend[g * LANES : (g + 1) * LANES, :] = dot(pick, grot[...]).astype(BF16)


def restore(z, dcol, brecv):
    owner, _ = split_pos(z, dcol[...])
    mine = iota((z.rows, z.peers), 1) == owner
    before = to_bf(iota((z.rows, z.rows), 1) < iota((z.rows, z.rows), 0))
    counts = dot(before, to_bf(mine))
    rank = jnp.sum(jnp.where(mine, counts, 0.0), axis=1, keepdims=True).astype(jnp.int32)
    pick = to_bf(iota((z.rows, z.slots), 1) == owner * z.cap + rank)
    return dot(pick, brecv[...])


class GainSum:
    def __init__(self, z, own, refs, sems):
        self.z, self.own = z, own
        self.a, self.b, self.c, self.ta, self.tb = refs
        self.sems = sems
        s = lax.axis_index("sample")
        self.l = lax.axis_index("leaf")
        self.pair = {"sample": s + 1 - 2 * (s % 2)}
        self.cross = {"sample": (s + 2) % 4}

    def copy(self, src, dst, i, j, device):
        return pltpu.make_async_remote_copy(
            src_ref=src, dst_ref=dst, send_sem=self.sems[0].at[i], recv_sem=self.sems[1].at[j],
            device_id=device, device_id_type=MESH,
        )

    def step1(self):
        return self.copy(self.own, self.a, 0, 0, self.pair)

    def step2(self):
        return self.copy(self.ta, self.b, 1, 1, self.cross)

    def step3(self, d):
        there = (self.l + d) % self.z.leaf
        device = {"leaf": there}
        return (
            self.copy(self.tb, self.c.at[self.l], 2 + d, 2 + self.l, device),
            self.copy(self.tb, self.c.at[there], 2 + d, 2 + there, device),
        )

    def start1(self):
        self.step1().start()

    def start2(self):
        self.step1().wait_recv()
        self.ta[...] = self.own[...] + self.a[...]
        self.step2().start()

    def start3(self):
        self.step2().wait_recv()
        self.tb[...] = self.ta[...] + self.b[...]
        self.c[self.l] = self.tb[...]

        def body(d, carry):
            self.step3(d)[0].start()
            return carry

        lax.fori_loop(1, self.z.leaf, body, 0)

    def finish(self):
        def body(d, carry):
            self.step3(d)[1].wait_recv()
            return carry

        lax.fori_loop(1, self.z.leaf, body, 0)
        total = self.c[0]
        for j in range(1, self.z.leaf):
            total = total + self.c[j]
        return total

    def sent(self):
        self.step1().wait_send()
        self.step2().wait_send()

        def body(d, carry):
            self.step3(d)[0].wait_send()
            return carry

        lax.fori_loop(1, self.z.leaf, body, 0)


def gain_scratch(z):
    f = z.feat
    return [
        pltpu.VMEM((8, f), F32),
        pltpu.VMEM((8, f), F32),
        pltpu.VMEM((z.leaf, 8, f), F32),
        pltpu.VMEM((8, f), F32),
        pltpu.VMEM((8, f), F32),
    ]


def gain_sems(z):
    return [pltpu.SemaphoreType.DMA((2 + z.leaf,)), pltpu.SemaphoreType.DMA((2 + z.leaf,))]


def write_outputs(z, fams, gsum, o_qkv, o_out, o_up, o_down, o_g1, o_g2):
    up, down, qo = fams
    f = z.feat
    inv = z.inv_root
    for s in range(z.sample):
        o_up[:, s * f : (s + 1) * f] = up.fourth[s].astype(F32) * inv
        o_down[s * z.down : (s + 1) * z.down, :] = down.fourth[s].astype(F32) * inv
    for s in range(3):
        o_qkv[:, s * f : (s + 1) * f] = qo.fourth[s].astype(F32) * inv
    o_out[...] = qo.fourth[3].astype(F32) * inv
    me = lax.axis_index("leaf")
    for o, r in ((o_g1, 0), (o_g2, 1)):
        acc = jnp.zeros((1, z.block), F32)
        for j in range(z.leaf):
            acc = jnp.where(me == j, gsum[r : r + 1, j * z.block : (j + 1) * z.block], acc)
        o[...] = acc * inv


def reduce_kernel(z, dcol, trecv, grot, up, down, qo, gains, *refs):
    o_pts, o_qkv, o_out, o_up, o_down, o_g1, o_g2 = refs[:7]
    refs = refs[7:]
    fr = [refs[7 * i : 7 * i + 7] for i in range(3)]
    refs = refs[21:]
    gr, refs = refs[:5], refs[5:]
    bsend, brecv = refs[:2]
    refs = refs[2:]
    fs = [refs[2 * i : 2 * i + 2] for i in range(3)]
    gs, bs = refs[6:8], refs[8:10]
    fams = [Family(z, own, r, s) for own, r, s in zip((up, down, qo), fr, fs)]
    gain = GainSum(z, gains, gr, gs)
    greet_all(z)
    gain.start1()
    for f in fams:
        f.start1()
    back_rows(z, trecv, grot, bsend)
    keep_own(z, bsend, brecv, z.cap)
    swap_start(z, bsend, brecv, bs, z.cap)
    gain.start2()
    for f in fams:
        f.start2()
    gain.start3()
    for f in fams:
        f.start3()
    for f in fams:
        f.start4()
    total = gain.finish()
    swap_recv(z, bsend, brecv, bs, z.cap)
    o_pts[...] = restore(z, dcol, brecv).astype(BF16)
    for f in fams:
        f.finish()
    write_outputs(z, fams, total, o_qkv, o_out, o_up, o_down, o_g1, o_g2)
    gain.sent()
    for f in fams:
        f.sent()
    swap_sent(z, bsend, brecv, bs, z.cap)


def call(kernel, outs, scratch, collective):
    vmem = pl.BlockSpec(memory_space=pltpu.VMEM)

    def run(*args):
        options = dict(vmem_limit_bytes=48 * 1024 * 1024)
        if collective is not None:
            options.update(collective_id=collective, has_side_effects=True)
        return pl.pallas_call(
            kernel,
            out_shape=[jax.ShapeDtypeStruct(s, t) for s, t in outs],
            in_specs=[vmem] * len(args),
            out_specs=[vmem] * len(outs),
            scratch_shapes=scratch,
            compiler_params=pltpu.CompilerParams(**options),
        )(*args)

    return run


def swap_sems(z):
    return [pltpu.SemaphoreType.DMA((z.peers,)), pltpu.SemaphoreType.DMA((z.peers,))]


def layer_scratch(z):
    r, f = z.rows, z.feat
    balls = r // BALL
    return [
        pltpu.VMEM((r, 3 * f), BF16),
        pltpu.VMEM((HEADS * balls, BALL, BALL), F32),
        pltpu.VMEM((r, f), BF16),
        pltpu.VMEM((r, f), BF16),
        pltpu.VMEM((r, 3 * f), BF16),
        pltpu.VMEM((balls, f, BALL), BF16),
        pltpu.VMEM((balls, f, BALL), BF16),
        pltpu.VMEM((balls, f, BALL), F32),
        pltpu.VMEM((balls, f, BALL), F32),
    ]


def local(mesh, points, cotangent, dest_pos, w_qkv, w_out, w_up, w_down, gain_attn, gain_mlp):
    rows, feat = points.shape
    z = Sizes(mesh, rows, feat, w_up.shape[1])
    drow = dest_pos.reshape(1, rows)
    dcol = dest_pos.reshape(rows, 1)
    trow = (z.peers, 1, LANES)
    rot, rcot, trecv = call(
        lambda *r: dispatch_kernel(z, *r),
        [((rows, feat), BF16), ((rows, feat), BF16), (trow, F32)],
        [
            pltpu.VMEM((z.slots, rows), BF16),
            pltpu.VMEM(trow, F32),
            pltpu.VMEM((z.slots, feat), BF16),
            pltpu.VMEM((z.slots, feat), BF16),
            pltpu.VMEM((z.slots, feat), BF16),
            pltpu.VMEM((z.slots, feat), BF16),
        ]
        + swap_sems(z) * 3,
        0,
    )(drow, points, cotangent)
    fam = ((z.sample, feat, feat), z.wire)
    grot, up, down, qo, gains = call(
        lambda *r: layer_kernel(z, *r),
        [((rows, feat), BF16), fam, fam, fam, ((8, feat), F32)],
        layer_scratch(z),
        None,
    )(
        rot, rcot, w_qkv, w_out, w_up, w_down,
        gain_attn.reshape(1, feat), gain_mlp.reshape(1, feat),
    )
    o_pts, o_qkv, o_out, o_up, o_down, o_g1, o_g2 = call(
        lambda *r: reduce_kernel(z, *r),
        [
            ((rows, feat), BF16),
            ((z.block, 3 * feat), F32),
            ((z.block, feat), F32),
            ((z.block, z.hid), F32),
            ((z.hid // z.leaf, feat), F32),
            ((1, z.block), F32),
            ((1, z.block), F32),
        ],
        family_scratch(z) * 3
        + gain_scratch(z)
        + [pltpu.VMEM((z.slots, feat), BF16), pltpu.VMEM((z.slots, feat), BF16)]
        + family_sems(z) * 3
        + gain_sems(z)
        + swap_sems(z),
        1,
    )(dcol, trecv, grot, up, down, qo, gains)
    return (o_pts, o_qkv, o_out, o_up, o_down, o_g1.reshape(z.block), o_g2.reshape(z.block))


def solution(mesh):
    rows = P(("groups", "leaf", "sample"), None)
    leaf = P(("groups", "leaf"), None)
    in_specs = (rows, rows, P(("groups", "leaf", "sample"))) + (P(),) * 6
    out_specs = (rows,) + (leaf,) * 4 + (P(("groups", "leaf")),) * 2
    return jax.shard_map(
        lambda *a: local(mesh, *a),
        mesh=mesh,
        in_specs=in_specs,
        out_specs=out_specs,
        check_vma=False,
    )
```

time: 250 us -> 93 us (0.37)
  waiting for transfers between devices: 122 us -> 0 us
  Pallas kernels: 0 us -> 81.4 us
  matrix products: 26.9 us -> 0 us
  local copies, waits for them, and re-layouts: 36.2 us -> 10.6 us
  starting transfers between devices: 19.6 us -> 0 us
  blocking collectives: 15.4 us -> 0 us
  other arithmetic: 14.5 us -> 0 us
  between operations: 15 us -> 0.72 us
    reduce_scatter x4 -> x0, waiting for transfers between devices: 83.8 us -> none  [the longest x1 29.9 us: local(): lax.psum_scatter(grad_down, 'leaf', scatter_dimension=0, tiled=True)]
    pallas_call x0 -> x3, Pallas kernels: none -> 81.4 us  [run(): pl.pallas_call(kernel, out_shape=[jax.ShapeDtypeStruct(s, t) for s, t in...]
    dot_general x16 -> x0, matrix products: 23.4 us -> none  [the longest x1 3.77 us: ball_backward(): jnp.einsum('ghqk,gqhd->gkhd', probs_low, upstream, preferred_element_type...]
    all_to_all x4 -> x0, waiting for transfers between devices: 21.6 us -> none  [the longest x1 10.9 us: local(): lax.all_to_all(send_points.reshape(peer_count, capacity, feat_width), ('l...]
    scatter x7 -> x0, local copies, waits for them, and re-layouts: 19.9 us -> none  [the longest x2 7.08 us: local(): jnp.zeros((peer_count * capacity, feat_width), jnp.bfloat16).at[slot_index]]
    all_to_all x4 -> x0, starting transfers between devices: 19.2 us -> none  [the longest x1 7.36 us: local(): lax.all_to_all(send_target.reshape(peer_count, capacity), ('leaf', 'sampl...]
    psum x1 -> x0, waiting for transfers between devices: 16.4 us -> none  [local(): lax.psum((shares[0], shares[1], shares[2], shares[3], shares[4], shares[5...]
    unnamed x1 -> x0, blocking collectives: 9.39 us -> none
  transfers between devices with their start and end apart: 9 -> 0, of which waited for: 7 -> 0; matrix products, arithmetic and copies ran while one was open for 15% -> 0% of each run, Pallas kernels for 0% -> 0%
where the time goes in v1:
time: 93 us; the launch traced here: 92.7 us
  Pallas kernels  81.4 us (88%)
  local copies, waits for them, and re-layouts  10.6 us (11%)
    pallas_call x3, Pallas kernels, run(): pl.pallas_call(kernel, out_shape=[jax.ShapeDtypeStruct(s, t) for s, t in...  81.4 us
    unnamed x25, local copies, waits for them, and re-layouts  9.71 us

profile of v1, /device:TPU:0, one launch (start us, length us, event | category | flops | bytes accessed | tf_op | source)
XLA Modules:
  0.0 92.7 jit_solution(7999692424011447726)
XLA Ops:
  0.6 0.0 copy-start
  0.6 0.9 copy.16.r_0_
  1.5 0.0 copy-start.3
  1.5 0.9 %copy-done.3 = bf16[512,256]{1,0:T(8,128)(2,1)S(1)} copy-done((bf16[512,256]{1,0:T(8,128)(2,1)S(1)}, bf16[512,256]{1,0:T(8,128)(2,1)}, u32[]{:S(2)}) %copy-start.3) | copy-done | bytes 262168
  2.5 0.0 copy-start.4
  2.5 0.9 %copy-done.4 = bf16[512,256]{1,0:T(8,128)(2,1)S(1)} copy-done((bf16[512,256]{1,0:T(8,128)(2,1)S(1)}, bf16[512,256]{1,0:T(8,128)(2,1)}, u32[]{:S(2)}) %copy-start.4) | copy-done | bytes 262168
  3.4 0.0 copy-start.6
  3.4 0.7 copy-done.6
  4.1 0.0 copy-start.5
  4.1 0.0 copy-start.8
  4.1 29.1 %shard_map.144 = (bf16[512,256]{1,0:T(8,128)(2,1)S(1)}, bf16[512,256]{1,0:T(8,128)(2,1)S(1)}, f32[16,1,256]{2,1,0:T(1,128)S(1)}) custom-call(s32[1,512]{1,0:T(1,128)S(1)} %bitcast.7, bf16[512,256]{1,0:T(8,128)(2,1)S(1)} %copy-done.3, bf16[512,256]{1,0:T(8,128)(2,1)S(1)} %copy-done.4), custom_call_target="tpu_custom_call" | custom-call | tf_op jit(solution)/shard_map/pallas_call | solution.py:643
  33.3 0.0 copy-start.7
  33.3 0.0 copy-done
  33.3 0.0 copy-done.5
  33.3 0.0 copy-done.8
  33.3 0.6 copy-done.7
  34.0 0.0 copy-start.1
  34.0 1.0 %copy-done.1 = bf16[1024,256]{1,0:T(8,128)(2,1)S(1)} copy-done((bf16[1024,256]{1,0:T(8,128)(2,1)S(1)}, bf16[1024,256]{1,0:T(8,128)(2,1)}, u32[]{:S(2)}) %copy-start.1) | copy-done | bytes 524312
  35.0 0.0 copy-start.2
  35.0 1.0 %copy-done.2 = bf16[256,768]{1,0:T(8,128)(2,1)S(1)} copy-done((bf16[256,768]{1,0:T(8,128)(2,1)S(1)}, bf16[256,768]{1,0:T(8,128)(2,1)}, u32[]{:S(2)}) %copy-start.2) | copy-done | bytes 393240
  36.0 18.5 %shard_map.145 = (bf16[512,256]{1,0:T(8,128)(2,1)S(1)}, bf16[4,256,256]{2,1,0:T(8,128)(2,1)S(1)}, bf16[4,256,256]{2,1,0:T(8,128)(2,1)S(1)}, bf16[4,256,256]{2,1,0:T(8,128)(2,1)S(1)}, f32[8,256]{1,0:T(8,128)S(1)}) custom-call(bf16[512,256]{1,0:T(8,128)(2,1)S(1)} %get-tuple-element.23.r_0_, bf16[512,256]{1,0:T(8,128)(2,1)S(1)} %get-tuple-element.24.r_1_, ...), custom_call_target="tpu_custom_call" | custom-call | tf_op jit(solution)/shard_map/pallas_call | solution.py:643
  54.5 33.8 %shard_map.146 = (bf16[512,256]{1,0:T(8,128)(2,1)S(1)}, f32[64,768]{1,0:T(8,128)S(1)}, f32[64,256]{1,0:T(8,128)S(1)}, f32[64,1024]{1,0:T(8,128)S(1)}, f32[256,25...) custom-call(s32[512,1]{1,0:T(8,128)S(1)} %copy.16.r_0_, f32[16,1,256]{2,1,0:T(1,128)S(1)} %get-tuple-element.22.r_1_, ...), custom_call_target="tpu_custom_call" | custom-call | tf_op jit(solution)/shard_map/pallas_call | solution.py:643
  88.3 0.7 copy.24
  89.0 0.7 copy.25
  89.7 0.6 copy.26
  90.3 0.7 copy.27
  91.0 0.7 copy.28
  91.7 0.5 copy.29
  92.2 0.5 copy.30
Async XLA Ops:
  0.6 32.7 %copy-start = (bf16[256,1024]{1,0:T(8,128)(2,1)S(1)}, bf16[256,1024]{1,0:T(8,128)(2,1)}, u32[]{:S(2)}) copy-start(bf16[256,1024]{1,0:T(8,128)(2,1)} %r_4_.1) | copy-start | bytes 1572868
  1.5 1.0 %copy-start.3 = (bf16[512,256]{1,0:T(8,128)(2,1)S(1)}, bf16[512,256]{1,0:T(8,128)(2,1)}, u32[]{:S(2)}) copy-start(bf16[512,256]{1,0:T(8,128)(2,1)} %r_1_.1) | copy-start | bytes 786436
  2.5 0.9 %copy-start.4 = (bf16[512,256]{1,0:T(8,128)(2,1)S(1)}, bf16[512,256]{1,0:T(8,128)(2,1)}, u32[]{:S(2)}) copy-start(bf16[512,256]{1,0:T(8,128)(2,1)} %r_2_.2) | copy-start | bytes 786436
  3.4 0.7 copy-start.6
  4.1 29.2 %copy-start.5 = (bf16[256,256]{1,0:T(8,128)(2,1)S(1)}, bf16[256,256]{1,0:T(8,128)(2,1)}, u32[]{:S(2)}) copy-start(bf16[256,256]{1,0:T(8,128)(2,1)} %r_3_.1) | copy-start | bytes 393220
  4.1 29.2 %copy-start.8 = (f32[256]{0:T(256)S(1)}, f32[256]{0:T(256)}, u32[]{:S(2)}) copy-start(f32[256]{0:T(256)} %param.17) | copy-start | bytes 3076
  33.3 0.7 copy-start.7
  34.0 1.0 %copy-start.1 = (bf16[1024,256]{1,0:T(8,128)(2,1)S(1)}, bf16[1024,256]{1,0:T(8,128)(2,1)}, u32[]{:S(2)}) copy-start(bf16[1024,256]{1,0:T(8,128)(2,1)} %r_5_.1) | copy-start | bytes 1572868
  35.0 1.0 %copy-start.2 = (bf16[256,768]{1,0:T(8,128)(2,1)S(1)}, bf16[256,768]{1,0:T(8,128)(2,1)}, u32[]{:S(2)}) copy-start(bf16[256,768]{1,0:T(8,128)(2,1)} %r_2_.3) | copy-start | bytes 1179652

commit v2 on v1

v2 whole, which is shorter than its diff:
```python
import math

import jax
import jax.numpy as jnp
from jax import lax
from jax.experimental import pallas as pl
from jax.experimental.pallas import tpu as pltpu
from jax.sharding import PartitionSpec as P

HEADS = 8
BALL = 256
HEAD_DIM = 32
EPSILON = 1e-06
GELU_COEF = math.sqrt(2.0 / math.pi)
LANES = 256
MESH = pl.DeviceIdType.MESH
F32 = jnp.float32
BF16 = jnp.bfloat16


class Sizes:
    def __init__(self, mesh, rows, feat, hid):
        self.leaf = mesh.shape["leaf"]
        self.sample = mesh.shape["sample"]
        self.peers = self.leaf * self.sample
        self.rows = rows
        self.feat = feat
        self.hid = hid
        self.cap = max(16, 2 * rows // self.peers)
        self.slots = self.peers * self.cap
        self.groups = self.slots // LANES
        self.block = feat // self.leaf
        self.wire = BF16 if self.block % 16 == 0 else F32
        self.down = hid // self.peers
        self.inv_root = 1.0 / math.sqrt(rows * self.peers)


def dot(a, b):
    return jnp.dot(a, b, preferred_element_type=F32)


def dot_nt(a, b):
    return lax.dot_general(a, b, (((1,), (1,)), ((), ())), preferred_element_type=F32)


def dot_tn(a, b):
    return lax.dot_general(a, b, (((0,), (0,)), ((), ())), preferred_element_type=F32)


def iota(shape, dim):
    return lax.broadcasted_iota(jnp.int32, shape, dim)


def to_bf(mask):
    return jnp.where(mask, 1.0, 0.0).astype(BF16)


def position(z):
    return lax.axis_index("leaf") * z.sample + lax.axis_index("sample")


def peer_id(z, p):
    return {"leaf": p // z.sample, "sample": p % z.sample}


def greet_all(z):
    me = position(z)
    barrier = pltpu.get_barrier_semaphore()

    def body(d, carry):
        pl.semaphore_signal(
            barrier, inc=1, device_id=peer_id(z, (me + d) % z.peers), device_id_type=MESH
        )
        return carry

    lax.fori_loop(1, z.peers, body, 0)


def greeted(z):
    pl.semaphore_wait(pltpu.get_barrier_semaphore(), z.peers - 1)


def view(z, ref, p, count):
    if count is None:
        return ref.at[p]
    return ref.at[pl.ds(pl.multiple_of(p * count, count), count)]


def swap_copy(z, src, dst, sems, d, there, here, to, count):
    return pltpu.make_async_remote_copy(
        src_ref=view(z, src, there, count),
        dst_ref=view(z, dst, here, count),
        send_sem=sems[0].at[d],
        recv_sem=sems[1].at[here],
        device_id=peer_id(z, to),
        device_id_type=MESH,
    )


def swap_start(z, src, dst, sems, count):
    me = position(z)

    def body(d, carry):
        p = (me + d) % z.peers
        swap_copy(z, src, dst, sems, d, p, me, p, count).start()
        return carry

    near = z.sample
    lax.fori_loop(near, z.peers, body, 0)
    lax.fori_loop(1, near, body, 0)


def swap_recv(z, src, dst, sems, count):
    me = position(z)

    def body(d, carry):
        q = (me + d) % z.peers
        swap_copy(z, src, dst, sems, d, q, q, q, count).wait_recv()
        return carry

    lax.fori_loop(1, z.peers, body, 0)


def swap_sent(z, src, dst, sems, count):
    me = position(z)

    def body(d, carry):
        q = (me + d) % z.peers
        swap_copy(z, src, dst, sems, d, q, q, q, count).wait_send()
        return carry

    lax.fori_loop(1, z.peers, body, 0)


def keep_own(z, src, dst, count):
    me = position(z)
    where = pl.ds(pl.multiple_of(me * count, count), count)
    dst[where, :] = src[where, :]


def split_pos(z, pos):
    bits = z.rows.bit_length() - 1
    return lax.shift_right_logical(pos, bits), jnp.bitwise_and(pos, z.rows - 1)


def prepare(z, pos, tsend, place):
    me = position(z)
    owner, target = split_pos(z, pos)
    mine = iota((z.peers, z.rows), 0) == owner
    before = to_bf(iota((z.rows, z.rows), 0) < iota((z.rows, z.rows), 1))
    counts = dot(to_bf(mine), before)
    rank = jnp.sum(jnp.where(mine, counts, 0.0), axis=0, keepdims=True).astype(jnp.int32)
    place[...] = to_bf(iota((z.slots, z.rows), 0) == owner * z.cap + rank)
    shift = (me % (LANES // z.cap)) * z.cap
    at_lane = to_bf(iota((LANES, z.rows), 0) == rank + shift)
    code = target + 1
    high = lax.shift_right_logical(code, 4).astype(F32)
    low = jnp.bitwise_and(code, 15).astype(F32)
    targets = 16.0 * dot_nt(jnp.where(mine, high, 0.0).astype(BF16), at_lane) + dot_nt(
        jnp.where(mine, low, 0.0).astype(BF16), at_lane
    )
    for p in range(z.peers):
        tsend[p] = targets[p : p + 1, :]


def group_targets(z, trecv, g):
    per = LANES // z.cap
    row = trecv[g * per]
    for j in range(1, per):
        row = row + trecv[g * per + j]
    return row


def group_picks(z, trecv, pick, back):
    for g in range(z.groups):
        row = group_targets(z, trecv, g)
        cols = slice(g * LANES, (g + 1) * LANES)
        pick[:, cols] = to_bf((iota((z.rows, LANES), 0) + 1).astype(F32) == row)
        col = jnp.broadcast_to(row, (128, LANES)).T[:, 0:1]
        back[cols, :] = to_bf((iota((LANES, z.rows), 1) + 1).astype(F32) == col)


def restore_pick(z, pos, restore):
    pos = jnp.broadcast_to(pos.astype(F32), (128, z.rows)).T[:, 0:1].astype(jnp.int32)
    owner, _ = split_pos(z, pos)
    mine = iota((z.rows, z.peers), 1) == owner
    before = to_bf(iota((z.rows, z.rows), 1) < iota((z.rows, z.rows), 0))
    counts = dot(before, to_bf(mine))
    rank = jnp.sum(jnp.where(mine, counts, 0.0), axis=1, keepdims=True).astype(jnp.int32)
    restore[...] = to_bf(iota((z.rows, z.slots), 1) == owner * z.cap + rank)


def scale_of(matrix):
    return lax.rsqrt(jnp.mean(matrix * matrix, axis=1, keepdims=True) + EPSILON)


def head_mask(feat, h, dim):
    shape = (1, feat) if dim == 1 else (feat, 1)
    return lax.shift_right_logical(iota(shape, dim), 5) == h


def attention_forward(z, qkv, probs, att):
    feat = z.feat
    balls = z.rows // BALL
    root = HEAD_DIM**-0.5

    def body(h, totals):
        mask = head_mask(feat, h, 1)
        out = []
        for b in range(balls):
            rows = slice(b * BALL, (b + 1) * BALL)
            zero = jnp.zeros((), BF16)
            q = jnp.where(mask, qkv[rows, 0:feat], zero)
            v = jnp.where(mask, qkv[rows, 2 * feat : 3 * feat], zero)
            scores = dot_nt(q, qkv[rows, feat : 2 * feat]) * root
            e = jnp.exp(scores - jnp.max(scores, axis=1, keepdims=True))
            p = e * (1.0 / jnp.sum(e, axis=1, keepdims=True))
            probs[h * balls + b] = p
            out.append(totals[b] + dot(p.astype(BF16), v))
        return tuple(out)

    start = tuple(jnp.zeros((BALL, feat), F32) for _ in range(balls))
    totals = lax.fori_loop(0, HEADS, body, start)
    for b in range(balls):
        att[b * BALL : (b + 1) * BALL, :] = totals[b].astype(BF16)


def mlp_forward(z, normed_two, w_up, hidden, slope):
    width = z.hid // z.sample
    for c in range(z.sample):
        cols = slice(c * width, (c + 1) * width)
        x = dot(normed_two, w_up[:, cols])
        x2 = x * x
        t = jnp.tanh(GELU_COEF * (x + 0.044715 * x2 * x))
        half = 0.5 * (1.0 + t)
        hidden[:, cols] = (x * half).astype(BF16)
        slope[:, cols] = half + 0.5 * x * (1.0 - t * t) * GELU_COEF * (
            1.0 + 3.0 * 0.044715 * x2
        )


def mlp_backward(z, rc, n2t, hidden, slope, w_up, w_down, up, down):
    total = None
    width = z.hid // z.sample
    per_leaf = z.hid // z.leaf
    for c in range(z.sample):
        cols = slice(c * width, (c + 1) * width)
        gpre = (dot_nt(rc, w_down[cols, :]) * slope[:, cols]).astype(BF16)
        up[c] = dot(n2t, gpre).astype(up.dtype)
        gdown = dot_tn(hidden[:, cols], rc).astype(down.dtype)
        for r in range(0, width, z.down):
            row = c * width + r
            leaf, inner = row // per_leaf, row % per_leaf
            s = inner // z.down
            down[s, leaf * z.down : (leaf + 1) * z.down, :] = gdown[r : r + z.down, :]
        part = dot_nt(gpre, w_up[:, cols])
        total = part if total is None else total + part
    return total


def attention_backward(z, qkv, probs, gatt, turned, lo, hi, totals):
    feat = z.feat
    balls = z.rows // BALL
    qt, gt, dkt, dvt = turned

    def body(h, totals):
        mask = head_mask(feat, h, 1)
        head_rows = pl.ds(pl.multiple_of(h * HEAD_DIM, HEAD_DIM), HEAD_DIM)
        out = []
        for b in range(balls):
            rows = slice(b * BALL, (b + 1) * BALL)
            zero = jnp.zeros((), BF16)
            g = jnp.where(mask, gatt[rows, :], zero)
            k = jnp.where(mask, qkv[rows, feat : 2 * feat], zero)
            p = probs[h * balls + b]
            gp = dot_nt(g, qkv[rows, 2 * feat : 3 * feat])
            delta = jnp.sum(gp * p, axis=1, keepdims=True)
            gs = (p * (gp - delta)).astype(BF16)
            out.append(totals[b] + dot(gs, k))
            dkt[b, head_rows, :] = dot(qt[b, head_rows, :], gs)
            dvt[b, head_rows, :] = dot(gt[b, head_rows, :], p.astype(BF16))
        return tuple(out)

    return lax.fori_loop(lo, hi, body, totals)


class Family:
    def __init__(self, z, own, refs, sems):
        self.z, self.own = z, own
        self.first, self.far, self.second, self.out3, self.third, self.out4, self.fourth = refs
        self.sems = sems
        self.s = lax.axis_index("sample")
        self.l = lax.axis_index("leaf")
        self.pair = self.s + 1 - 2 * (self.s % 2)
        self.cross = (self.s + 2) % 4

    def copy(self, src, dst, i, j, device):
        return pltpu.make_async_remote_copy(
            src_ref=src,
            dst_ref=dst,
            send_sem=self.sems[0].at[i],
            recv_sem=self.sems[1].at[j],
            device_id=device,
            device_id_type=MESH,
        )

    def step1(self):
        pair = {"sample": self.pair}
        return [
            self.copy(self.own.at[(self.pair + 2) % 4], self.first.at[1], 1, 1, pair),
            self.copy(self.own.at[self.pair], self.first.at[0], 0, 0, pair),
        ]

    def start1(self):
        for c in self.step1():
            c.start()

    def step2(self):
        return self.copy(self.far, self.second, 2, 2, {"sample": self.cross})

    def start2(self):
        far, near = self.step1()
        far.wait_recv()
        total = self.own[self.cross].astype(F32) + self.first[1].astype(F32)
        self.far[...] = total.astype(self.far.dtype)
        self.step2().start()
        near.wait_recv()

    def step3(self, d, source=None):
        z = self.z
        there = (self.l + d) % z.leaf
        slot = self.l if source is None else there
        rows = pl.ds(pl.multiple_of(there * z.block, z.block), z.block)
        return self.copy(
            self.out3.at[rows], self.third.at[slot], 3 + d, 3 + slot, {"leaf": there}
        )

    def start3(self):
        self.step2().wait_recv()
        total = (
            self.own[self.s].astype(F32) + self.first[0].astype(F32) + self.second[...].astype(F32)
        )
        self.out3[...] = total.astype(self.out3.dtype)

        def body(d, carry):
            self.step3(d).start()
            return carry

        lax.fori_loop(1, self.z.leaf, body, 0)

    def step4(self, d, source=None):
        z = self.z
        there = (self.s + d) % z.sample
        slot = self.s if source is None else there
        base = 3 + z.leaf
        return self.copy(self.out4, self.fourth.at[slot], base + d, base + slot, {"sample": there})

    def start4(self):
        z = self.z

        def body(d, carry):
            self.step3(d, 1).wait_recv()
            return carry

        lax.fori_loop(1, z.leaf, body, 0)
        rows = pl.ds(pl.multiple_of(self.l * z.block, z.block), z.block)
        self.third[self.l] = self.out3[rows, :]
        total = self.third[0].astype(F32)
        for j in range(1, z.leaf):
            total = total + self.third[j].astype(F32)
        self.out4[...] = total.astype(self.out4.dtype)
        self.fourth[self.s] = self.out4[...]
        for d in range(1, z.sample):
            self.step4(d).start()

    def finish(self):
        for d in range(1, self.z.sample):
            self.step4(d, 1).wait_recv()

    def sent(self):
        for c in self.step1():
            c.wait_send()
        self.step2().wait_send()

        def body(d, carry):
            self.step3(d).wait_send()
            return carry

        lax.fori_loop(1, self.z.leaf, body, 0)
        for d in range(1, self.z.sample):
            self.step4(d).wait_send()


def family_scratch(z):
    f, w = z.feat, z.wire
    return [
        pltpu.VMEM((2, f, f), w),
        pltpu.VMEM((f, f), w),
        pltpu.VMEM((f, f), w),
        pltpu.VMEM((f, f), w),
        pltpu.VMEM((z.leaf, z.block, f), w),
        pltpu.VMEM((z.block, f), w),
    ]


def family_sems(z):
    count = 3 + z.leaf + z.sample
    return [pltpu.SemaphoreType.DMA((count,)), pltpu.SemaphoreType.DMA((count,))]


class GainSum:
    def __init__(self, z, own, refs, sems):
        self.z, self.own = z, own
        self.a, self.b, self.c, self.ta, self.tb = refs
        self.sems = sems
        s = lax.axis_index("sample")
        self.l = lax.axis_index("leaf")
        self.pair = {"sample": s + 1 - 2 * (s % 2)}
        self.cross = {"sample": (s + 2) % 4}

    def copy(self, src, dst, i, j, device):
        return pltpu.make_async_remote_copy(
            src_ref=src, dst_ref=dst, send_sem=self.sems[0].at[i], recv_sem=self.sems[1].at[j],
            device_id=device, device_id_type=MESH,
        )

    def step1(self):
        return self.copy(self.own, self.a, 0, 0, self.pair)

    def step2(self):
        return self.copy(self.ta, self.b, 1, 1, self.cross)

    def step3(self, d, source=None):
        there = (self.l + d) % self.z.leaf
        slot = self.l if source is None else there
        return self.copy(self.tb, self.c.at[slot], 2 + d, 2 + slot, {"leaf": there})

    def start1(self):
        self.step1().start()

    def start2(self):
        self.step1().wait_recv()
        self.ta[...] = self.own[...] + self.a[...]
        self.step2().start()

    def start3(self):
        self.step2().wait_recv()
        self.tb[...] = self.ta[...] + self.b[...]
        self.c[self.l] = self.tb[...]

        def body(d, carry):
            self.step3(d).start()
            return carry

        lax.fori_loop(1, self.z.leaf, body, 0)

    def finish(self):
        def body(d, carry):
            self.step3(d, 1).wait_recv()
            return carry

        lax.fori_loop(1, self.z.leaf, body, 0)
        total = self.c[0]
        for j in range(1, self.z.leaf):
            total = total + self.c[j]
        return total

    def sent(self):
        self.step1().wait_send()
        self.step2().wait_send()

        def body(d, carry):
            self.step3(d).wait_send()
            return carry

        lax.fori_loop(1, self.z.leaf, body, 0)


def gain_scratch(z):
    f = z.feat
    return [
        pltpu.VMEM((8, f), F32),
        pltpu.VMEM((8, f), F32),
        pltpu.VMEM((z.leaf, 8, f), F32),
        pltpu.VMEM((8, f), F32),
        pltpu.VMEM((8, f), F32),
    ]


def gain_sems(z):
    return [pltpu.SemaphoreType.DMA((2 + z.leaf,)), pltpu.SemaphoreType.DMA((2 + z.leaf,))]


class Take:
    def __init__(self, items):
        self.items = list(items)

    def __call__(self, count):
        head, self.items = self.items[:count], self.items[count:]
        return head


def fused_kernel(z, *refs):
    take = Take(refs)
    drow, gain_attn, gain_mlp = take(3)
    outside = take(6)
    o_pts, up_fourth, down_fourth, qo_fourth, gsum = take(5)
    pts, cot, w_qkv, w_out, w_up, w_down = inside = take(6)
    fr = [take(6) + [last] for last in (up_fourth, down_fourth, qo_fourth)]
    gr = take(5)
    up, down, qo, gains = take(4)
    place, pick, back, restore = take(4)
    tsend, trecv, psend, csend, precv, crecv, bsend, brecv = take(8)
    qkv, probs, att, gatt, gqkv, qt, gt, dkt, dvt, hidden, slope = take(11)
    fs = [take(2) for _ in range(3)]
    gs, ts, ps, cs, bs = take(2), take(2), take(2), take(2), take(2)
    (ls,) = take(1)
    loads = [pltpu.make_async_copy(a, b, ls.at[i]) for i, (a, b) in enumerate(zip(outside, inside))]

    me = position(z)
    feat = z.feat
    balls = z.rows // BALL
    root = HEAD_DIM**-0.5
    fams = [Family(z, own, r, s) for own, r, s in zip((up, down, qo), fr, fs)]
    fup, fdown, fqo = fams
    gain = GainSum(z, gains, gr, gs)

    greet_all(z)
    for load in loads:
        load.start()
    pos = drow[...]
    prepare(z, pos, tsend, place)
    trecv[me] = tsend[me]
    loads[0].wait()
    psend[...] = dot(place[...], pts[...]).astype(BF16)
    greeted(z)
    swap_start(z, tsend, trecv, ts, None)
    swap_start(z, psend, precv, ps, z.cap)
    loads[1].wait()
    csend[...] = dot(place[...], cot[...]).astype(BF16)
    swap_start(z, csend, crecv, cs, z.cap)
    keep_own(z, psend, precv, z.cap)
    keep_own(z, csend, crecv, z.cap)
    restore_pick(z, pos, restore)
    swap_recv(z, tsend, trecv, ts, None)
    group_picks(z, trecv, pick, back)
    for load in loads[2:]:
        load.wait()
    swap_recv(z, psend, precv, ps, z.cap)

    rotated = dot(pick[...], precv[...])
    scale_one = scale_of(rotated)
    norm_one = rotated * scale_one
    normed_one = (norm_one * gain_attn[...]).astype(BF16)
    qkv[...] = dot(normed_one, w_qkv[...]).astype(BF16)
    attention_forward(z, qkv, probs, att)
    middle = rotated + dot(att[...], w_out[...])
    scale_two = scale_of(middle)
    norm_two = middle * scale_two
    normed_two = (norm_two * gain_mlp[...]).astype(BF16)
    mlp_forward(z, normed_two, w_up, hidden, slope)
    n2t = normed_two.T
    n1t = normed_one.T
    for b in range(balls):
        qt[b] = qkv[b * BALL : (b + 1) * BALL, 0:feat].T

    swap_recv(z, csend, crecv, cs, z.cap)
    rcf = dot(pick[...], crecv[...])
    gn2 = mlp_backward(z, rcf.astype(BF16), n2t, hidden, slope, w_up, w_down, up, down)
    fup.start1()
    fdown.start1()
    gains[...] = jnp.zeros((8, feat), F32)
    gains[1:2, :] = jnp.sum(gn2 * norm_two, axis=0, keepdims=True)
    inner_two = gn2 * gain_mlp[...]
    gmid = rcf + scale_two * (
        inner_two - norm_two * jnp.mean(inner_two * norm_two, axis=1, keepdims=True)
    )
    gmid_low = gmid.astype(BF16)
    qo[3] = dot_tn(att[...], gmid_low).astype(qo.dtype)
    gatt[...] = dot_nt(gmid_low, w_out[...]).astype(BF16)
    for b in range(balls):
        gt[b] = gatt[b * BALL : (b + 1) * BALL, :].T
    totals = tuple(jnp.zeros((BALL, feat), F32) for _ in range(balls))
    turned = (qt, gt, dkt, dvt)
    totals = attention_backward(z, qkv, probs, gatt, turned, 0, HEADS // 2, totals)
    fup.start2()
    fdown.start2()
    totals = attention_backward(z, qkv, probs, gatt, turned, HEADS // 2, HEADS, totals)
    fup.start3()
    fdown.start3()
    for b in range(balls):
        rows = slice(b * BALL, (b + 1) * BALL)
        gqkv[rows, 0:feat] = (totals[b] * root).astype(BF16)
        gqkv[rows, feat : 2 * feat] = (dkt[b] * root).astype(BF16).T
        gqkv[rows, 2 * feat : 3 * feat] = dvt[b].astype(BF16).T
    gn1 = dot_nt(gqkv[...], w_qkv[...])
    gains[0:1, :] = jnp.sum(gn1 * norm_one, axis=0, keepdims=True)
    inner_one = gn1 * gain_attn[...]
    grot = (
        gmid
        + scale_one * (inner_one - norm_one * jnp.mean(inner_one * norm_one, axis=1, keepdims=True))
    ).astype(BF16)
    bsend[...] = dot(back[...], grot).astype(BF16)
    swap_start(z, bsend, brecv, bs, z.cap)
    for c in range(3):
        qo[c] = dot(n1t, gqkv[:, c * feat : (c + 1) * feat]).astype(qo.dtype)
    fqo.start1()
    gain.start1()
    keep_own(z, bsend, brecv, z.cap)
    fup.start4()
    fdown.start4()
    fqo.start2()
    gain.start2()
    fqo.start3()
    gain.start3()
    fqo.start4()
    gsum[...] = gain.finish()
    swap_recv(z, bsend, brecv, bs, z.cap)
    o_pts[...] = dot(restore[...], brecv[...]).astype(BF16)
    for f in fams:
        f.finish()
    for f in fams:
        f.sent()
    gain.sent()
    swap_sent(z, tsend, trecv, ts, None)
    swap_sent(z, psend, precv, ps, z.cap)
    swap_sent(z, csend, crecv, cs, z.cap)
    swap_sent(z, bsend, brecv, bs, z.cap)


def finish_kernel(z, pts, up, down, qo, gsum, o_pts, o_qkv, o_out, o_up, o_down, o_g1, o_g2):
    f = z.feat
    inv = z.inv_root
    o_pts[...] = pts[...]
    for s in range(z.sample):
        o_up[:, s * f : (s + 1) * f] = up[s].astype(F32) * inv
        o_down[s * z.down : (s + 1) * z.down, :] = down[s].astype(F32) * inv
    for s in range(3):
        o_qkv[:, s * f : (s + 1) * f] = qo[s].astype(F32) * inv
    o_out[...] = qo[3].astype(F32) * inv
    me = lax.axis_index("leaf")
    for o, r in ((o_g1, 0), (o_g2, 1)):
        acc = jnp.zeros((1, z.block), F32)
        for j in range(z.leaf):
            acc = jnp.where(me == j, gsum[r : r + 1, j * z.block : (j + 1) * z.block], acc)
        o[...] = acc * inv


def call(kernel, outs, scratch, collective, near=None):
    vmem = pl.BlockSpec(memory_space=pltpu.VMEM)
    far = pl.BlockSpec(memory_space=pl.ANY)

    def run(*args):
        count = len(args) if near is None else near
        options = {}
        if collective is not None:
            options = dict(
                vmem_limit_bytes=48 * 1024 * 1024, collective_id=collective, has_side_effects=True
            )
        return pl.pallas_call(
            kernel,
            out_shape=[jax.ShapeDtypeStruct(s, t) for s, t in outs],
            in_specs=[vmem] * count + [far] * (len(args) - count),
            out_specs=[vmem] * len(outs),
            scratch_shapes=scratch,
            compiler_params=pltpu.CompilerParams(**options),
        )(*args)

    return run


def swap_sems(z):
    return [pltpu.SemaphoreType.DMA((z.peers,)), pltpu.SemaphoreType.DMA((z.peers,))]


def layer_scratch(z):
    r, f = z.rows, z.feat
    balls = r // BALL
    return [
        pltpu.VMEM((r, 3 * f), BF16),
        pltpu.VMEM((HEADS * balls, BALL, BALL), F32),
        pltpu.VMEM((r, f), BF16),
        pltpu.VMEM((r, f), BF16),
        pltpu.VMEM((r, 3 * f), BF16),
        pltpu.VMEM((balls, f, BALL), BF16),
        pltpu.VMEM((balls, f, BALL), BF16),
        pltpu.VMEM((balls, f, BALL), F32),
        pltpu.VMEM((balls, f, BALL), F32),
        pltpu.VMEM((r, z.hid), BF16),
        pltpu.VMEM((r, z.hid), F32),
    ]


def local(mesh, points, cotangent, dest_pos, w_qkv, w_out, w_up, w_down, gain_attn, gain_mlp):
    rows, feat = points.shape
    z = Sizes(mesh, rows, feat, w_up.shape[1])
    trow = (z.peers, 1, LANES)
    fam = (z.sample, feat, feat)
    last = ((z.sample, z.block, feat), z.wire)
    outside = (points, cotangent, w_qkv, w_out, w_up, w_down)
    slots = pltpu.VMEM((z.slots, feat), BF16)
    scratch = (
        [pltpu.VMEM(a.shape, a.dtype) for a in outside]
        + family_scratch(z) * 3
        + gain_scratch(z)
        + [pltpu.VMEM(fam, z.wire)] * 3
        + [pltpu.VMEM((8, feat), F32)]
        + [pltpu.VMEM(s, BF16) for s in ((z.slots, rows), (rows, z.slots)) * 2]
        + [pltpu.VMEM(trow, F32)] * 2
        + [slots] * 6
        + layer_scratch(z)
        + family_sems(z) * 3
        + gain_sems(z)
        + swap_sems(z) * 4
        + [pltpu.SemaphoreType.DMA((len(outside),))]
    )
    parts = call(
        lambda *r: fused_kernel(z, *r),
        [((rows, feat), BF16), last, last, last, ((8, feat), F32)],
        scratch,
        0,
        3,
    )(
        dest_pos.reshape(1, rows), gain_attn.reshape(1, feat), gain_mlp.reshape(1, feat), *outside
    )
    o_pts, o_qkv, o_out, o_up, o_down, o_g1, o_g2 = call(
        lambda *r: finish_kernel(z, *r),
        [
            ((rows, feat), BF16),
            ((z.block, 3 * feat), F32),
            ((z.block, feat), F32),
            ((z.block, z.hid), F32),
            ((z.hid // z.leaf, feat), F32),
            ((1, z.block), F32),
            ((1, z.block), F32),
        ],
        [],
        None,
    )(*parts)
    return (o_pts, o_qkv, o_out, o_up, o_down, o_g1.reshape(z.block), o_g2.reshape(z.block))


def solution(mesh):
    rows = P(("groups", "leaf", "sample"), None)
    leaf = P(("groups", "leaf"), None)
    in_specs = (rows, rows, P(("groups", "leaf", "sample"))) + (P(),) * 6
    out_specs = (rows,) + (leaf,) * 4 + (P(("groups", "leaf")),) * 2
    return jax.shard_map(
        lambda *a: local(mesh, *a),
        mesh=mesh,
        in_specs=in_specs,
        out_specs=out_specs,
        check_vma=False,
    )
```

time: 93 us -> 87.5 us (0.941)
  Pallas kernels: 81.4 us -> 76.6 us
    pallas_call x3 -> x2, Pallas kernels: 81.4 us -> 76.6 us  [run(): pl.pallas_call(kernel, out_shape=[jax.ShapeDtypeStruct(s, t) for s, t in...]
    unnamed x25 -> x28, local copies, waits for them, and re-layouts: 9.71 us -> 9.78 us
where the time goes in v2:
time: 87.5 us; the launch traced here: 87.1 us
  Pallas kernels  76.6 us (88%)
  local copies, waits for them, and re-layouts  9.78 us (11%)
    pallas_call x2, Pallas kernels, run(): pl.pallas_call(kernel, out_shape=[jax.ShapeDtypeStruct(s, t) for s, t in...  76.6 us
    unnamed x28, local copies, waits for them, and re-layouts  9.78 us

profile of v2, /device:TPU:0, one launch (start us, length us, event | category | flops | bytes accessed | tf_op | source)
XLA Modules:
  0.0 87.1 jit_solution(6107847371727418889)
XLA Ops:
  0.6 0.0 copy-start.13
  0.6 0.0 copy-start.11
  0.7 0.0 copy-start.12
  0.7 0.7 copy-done.13
  1.3 0.0 copy-done.11
  1.3 0.0 copy-done.12
  1.3 0.0 copy-start
  1.3 1.0 %copy-done = bf16[256,1024]{1,0:T(8,128)(2,1)S(1)} copy-done((bf16[256,1024]{1,0:T(8,128)(2,1)S(1)}, bf16[256,1024]{1,0:T(8,128)(2,1)}, u32[]{:S(2)}) %copy-start) | copy-done | bytes 524312
  2.4 0.0 copy-start.1
  2.4 1.0 %copy-done.1 = bf16[1024,256]{1,0:T(8,128)(2,1)S(1)} copy-done((bf16[1024,256]{1,0:T(8,128)(2,1)S(1)}, bf16[1024,256]{1,0:T(8,128)(2,1)}, u32[]{:S(2)}) %copy-start.1) | copy-done | bytes 524312
  3.4 0.0 copy-start.2
  3.4 1.0 %copy-done.2 = bf16[256,768]{1,0:T(8,128)(2,1)S(1)} copy-done((bf16[256,768]{1,0:T(8,128)(2,1)S(1)}, bf16[256,768]{1,0:T(8,128)(2,1)}, u32[]{:S(2)}) %copy-start.2) | copy-done | bytes 393240
  4.4 0.0 copy-start.4
  4.4 0.9 %copy-done.4 = bf16[512,256]{1,0:T(8,128)(2,1)S(1)} copy-done((bf16[512,256]{1,0:T(8,128)(2,1)S(1)}, bf16[512,256]{1,0:T(8,128)(2,1)}, u32[]{:S(2)}) %copy-start.4) | copy-done | bytes 262168
  5.4 0.0 copy-start.5
  5.4 0.9 %copy-done.5 = bf16[512,256]{1,0:T(8,128)(2,1)S(1)} copy-done((bf16[512,256]{1,0:T(8,128)(2,1)S(1)}, bf16[512,256]{1,0:T(8,128)(2,1)}, u32[]{:S(2)}) %copy-start.5) | copy-done | bytes 262168
  6.3 0.0 copy-start.6
  6.3 0.9 %copy-done.6 = bf16[256,256]{1,0:T(8,128)(2,1)S(1)} copy-done((bf16[256,256]{1,0:T(8,128)(2,1)S(1)}, bf16[256,256]{1,0:T(8,128)(2,1)}, u32[]{:S(2)}) %copy-start.6) | copy-done | bytes 131096
  7.2 74.3 %shard_map.144 = (bf16[512,256]{1,0:T(8,128)(2,1)S(1)}, bf16[4,64,256]{2,1,0:T(8,128)(2,1)S(1)}, bf16[4,64,256]{2,1,0:T(8,128)(2,1)S(1)}, bf16[4,64,256]{2,1,0:T(8,128)(2,1)S(1)}, f32[8,256]{1,0:T(8,128)S(1)}) custom-call(s32[1,512]{1,0:T(1,128)S(1)} %bitcast.5, f32[1,256]{1,0:T(1,128)S(1)} %bitcast.6, f32[1,256]{1,0:T(1,128)S(1)} %bitcast.7, ...), custom_call_target="tpu_custom_call" | custom-call | tf_op jit(solution)/shard_map/pallas_call | solution.py:660
  81.6 0.0 copy-start.3
  81.6 0.7 copy-done.3
  82.3 0.0 copy-start.7
  82.3 0.6 copy-done.7
  82.9 0.0 copy-start.8
  82.9 0.6 copy-done.8
  83.6 0.0 copy-start.9
  83.6 0.6 copy-done.9
  84.2 0.0 copy-start.10
  84.2 0.6 copy-done.10
  84.8 2.3 %shard_map.145 = (bf16[512,256]{1,0:T(8,128)(2,1)}, f32[64,768]{1,0:T(8,128)}, f32[64,256]{1,0:T(8,128)}, f32[64,1024]{1,0:T(8,128)}, f32[256,256]{1,0:T(8,128)}, /*index=5*/f32[1,64]{1,0:T(1,128)}, f32[1,64]{1,0:T(1,128)}) custom-call(bf16[512,256]{1,0:T(8,128)(2,1)} %copy-done.3, bf16[4,64,256]{2,1,0:T(8,128)(2,1)} %copy-done.7, ...), custom_call_target="tpu_custom_call" | custom-call | tf_op jit(solution)/shard_map/pallas_call | solution.py:660
Async XLA Ops:
  0.6 0.7 copy-start.13
  0.6 0.7 copy-start.11
  0.7 0.7 copy-start.12
  1.3 1.0 %copy-start = (bf16[256,1024]{1,0:T(8,128)(2,1)S(1)}, bf16[256,1024]{1,0:T(8,128)(2,1)}, u32[]{:S(2)}) copy-start(bf16[256,1024]{1,0:T(8,128)(2,1)} %r_7_.1) | copy-start | bytes 1572868
  2.4 1.0 %copy-start.1 = (bf16[1024,256]{1,0:T(8,128)(2,1)S(1)}, bf16[1024,256]{1,0:T(8,128)(2,1)}, u32[]{:S(2)}) copy-start(bf16[1024,256]{1,0:T(8,128)(2,1)} %r_8_.1) | copy-start | bytes 1572868
  3.4 1.0 %copy-start.2 = (bf16[256,768]{1,0:T(8,128)(2,1)S(1)}, bf16[256,768]{1,0:T(8,128)(2,1)}, u32[]{:S(2)}) copy-start(bf16[256,768]{1,0:T(8,128)(2,1)} %r_5_.1) | copy-start | bytes 1179652
  4.4 0.9 %copy-start.4 = (bf16[512,256]{1,0:T(8,128)(2,1)S(1)}, bf16[512,256]{1,0:T(8,128)(2,1)}, u32[]{:S(2)}) copy-start(bf16[512,256]{1,0:T(8,128)(2,1)} %r_3_.1) | copy-start | bytes 786436
  5.4 0.9 %copy-start.5 = (bf16[512,256]{1,0:T(8,128)(2,1)S(1)}, bf16[512,256]{1,0:T(8,128)(2,1)}, u32[]{:S(2)}) copy-start(bf16[512,256]{1,0:T(8,128)(2,1)} %r_4_.1) | copy-start | bytes 786436
  6.3 0.9 %copy-start.6 = (bf16[256,256]{1,0:T(8,128)(2,1)S(1)}, bf16[256,256]{1,0:T(8,128)(2,1)}, u32[]{:S(2)}) copy-start(bf16[256,256]{1,0:T(8,128)(2,1)} %r_6_.1) | copy-start | bytes 393220
  81.6 0.7 copy-start.3
  82.3 0.7 copy-start.7
  82.9 0.6 copy-start.8
  83.6 0.6 copy-start.9
  84.2 0.6 copy-start.10

commit v3 on v2

--- a/solution.py
+++ b/solution.py
@@ -13,6 +13,8 @@
 EPSILON = 1e-06
 GELU_COEF = math.sqrt(2.0 / math.pi)
 LANES = 256
+UNROLL = 4
+VMEM_BYTES = 63 * 1024 * 1024
 MESH = pl.DeviceIdType.MESH
 F32 = jnp.float32
 BF16 = jnp.bfloat16
@@ -220,7 +222,7 @@
         return tuple(out)
 
     start = tuple(jnp.zeros((BALL, feat), F32) for _ in range(balls))
-    totals = lax.fori_loop(0, HEADS, body, start)
+    totals = lax.fori_loop(0, HEADS, body, start, unroll=UNROLL)
     for b in range(balls):
         att[b * BALL : (b + 1) * BALL, :] = totals[b].astype(BF16)
 
@@ -281,7 +283,7 @@
             dvt[b, head_rows, :] = dot(gt[b, head_rows, :], p.astype(BF16))
         return tuple(out)
 
-    return lax.fori_loop(lo, hi, body, totals)
+    return lax.fori_loop(lo, hi, body, totals, unroll=UNROLL)
 
 
 class Family:
@@ -582,12 +584,7 @@
         gt[b] = gatt[b * BALL : (b + 1) * BALL, :].T
     totals = tuple(jnp.zeros((BALL, feat), F32) for _ in range(balls))
     turned = (qt, gt, dkt, dvt)
-    totals = attention_backward(z, qkv, probs, gatt, turned, 0, HEADS // 2, totals)
-    fup.start2()
-    fdown.start2()
-    totals = attention_backward(z, qkv, probs, gatt, turned, HEADS // 2, HEADS, totals)
-    fup.start3()
-    fdown.start3()
+    totals = attention_backward(z, qkv, probs, gatt, turned, 0, HEADS, totals)
     for b in range(balls):
         rows = slice(b * BALL, (b + 1) * BALL)
         gqkv[rows, 0:feat] = (totals[b] * root).astype(BF16)
@@ -602,17 +599,21 @@
     ).astype(BF16)
     bsend[...] = dot(back[...], grot).astype(BF16)
     swap_start(z, bsend, brecv, bs, z.cap)
+    fup.start2()
+    fdown.start2()
     for c in range(3):
         qo[c] = dot(n1t, gqkv[:, c * feat : (c + 1) * feat]).astype(qo.dtype)
     fqo.start1()
     gain.start1()
     keep_own(z, bsend, brecv, z.cap)
+    fqo.start2()
+    gain.start2()
+    fup.start3()
+    fdown.start3()
+    fqo.start3()
+    gain.start3()
     fup.start4()
     fdown.start4()
-    fqo.start2()
-    gain.start2()
-    fqo.start3()
-    gain.start3()
     fqo.start4()
     gsum[...] = gain.finish()
     swap_recv(z, bsend, brecv, bs, z.cap)
@@ -628,7 +629,17 @@
     swap_sent(z, bsend, brecv, bs, z.cap)
 
 
-def finish_kernel(z, pts, up, down, qo, gsum, o_pts, o_qkv, o_out, o_up, o_down, o_g1, o_g2):
+def finish_kernel(z, *refs):
+    outside, refs = refs[:5], refs[5:]
+    (o_pts, o_qkv, o_out, o_up, o_down, o_g1, o_g2), refs = refs[:7], refs[7:]
+    pts, up, down, qo, gsum = inside = refs[:5]
+    loads = [
+        pltpu.make_async_copy(a, b, refs[5].at[i]) for i, (a, b) in enumerate(zip(outside, inside))
+    ]
+    for load in loads:
+        load.start()
+    for load in loads:
+        load.wait()
     f = z.feat
     inv = z.inv_root
     o_pts[...] = pts[...]
@@ -648,15 +659,13 @@
 
 def call(kernel, outs, scratch, collective, near=None):
     vmem = pl.BlockSpec(memory_space=pltpu.VMEM)
-    far = pl.BlockSpec(memory_space=pl.ANY)
+    far = pl.BlockSpec(memory_space=pltpu.HBM)
 
     def run(*args):
         count = len(args) if near is None else near
-        options = {}
+        options = dict(vmem_limit_bytes=VMEM_BYTES)
         if collective is not None:
-            options = dict(
-                vmem_limit_bytes=48 * 1024 * 1024, collective_id=collective, has_side_effects=True
-            )
+            options.update(collective_id=collective, has_side_effects=True)
         return pl.pallas_call(
             kernel,
             out_shape=[jax.ShapeDtypeStruct(s, t) for s, t in outs],
@@ -734,8 +743,10 @@
             ((1, z.block), F32),
             ((1, z.block), F32),
         ],
-        [],
+        [pltpu.VMEM(a.shape, a.dtype) for a in parts]
+        + [pltpu.SemaphoreType.DMA((len(parts),))],
         None,
+        0,
     )(*parts)
     return (o_pts, o_qkv, o_out, o_up, o_down, o_g1.reshape(z.block), o_g2.reshape(z.block))
 

time: 87.5 us -> 71.3 us (0.81)
  local copies, waits for them, and re-layouts: 9.78 us -> 0 us
  Pallas kernels: 76.6 us -> 70.4 us
    unnamed x28 -> x0, local copies, waits for them, and re-layouts: 9.78 us -> none
    pallas_call x2, Pallas kernels: 76.6 us -> 70.4 us  [run(): pl.pallas_call(kernel, out_shape=[jax.ShapeDtypeStruct(s, t) for s, t in...]
where the time goes in v3:
time: 71.3 us; the launch traced here: 71.1 us
  Pallas kernels  70.4 us (99%)
    pallas_call x2, Pallas kernels, run(): pl.pallas_call(kernel, out_shape=[jax.ShapeDtypeStruct(s, t) for s, t in...  70.4 us

profile of v3, /device:TPU:0, one launch (start us, length us, event | category | flops | bytes accessed | tf_op | source)
XLA Modules:
  0.0 71.1 jit_solution(5567973360099218988)
XLA Ops:
  0.6 68.1 %shard_map.144 = (bf16[512,256]{1,0:T(8,128)(2,1)}, bf16[4,64,256]{2,1,0:T(8,128)(2,1)}, bf16[4,64,256]{2,1,0:T(8,128)(2,1)}, bf16[4,64,256]{2,1,0:T(8,128)(2,1)}, f32[8,256]{1,0:T(8,128)}) custom-call(s32[1,512]{1,0:T(1,128)} %bitcast.5, f32[1,256]{1,0:T(1,128)} %bitcast.6, f32[1,256]{1,0:T(1,128)} %bitcast.7, bf16[512,256]{1,0:T(8,128)(2,1)} %r_3_.1, ...), custom_call_target="tpu_custom_call" | custom-call | tf_op jit(solution)/shard_map/pallas_call | solution.py:669
  68.7 2.3 %shard_map.145 = (bf16[512,256]{1,0:T(8,128)(2,1)}, f32[64,768]{1,0:T(8,128)}, f32[64,256]{1,0:T(8,128)}, f32[64,1024]{1,0:T(8,128)}, f32[256,256]{1,0:T(8,128)}, /*index=5*/f32[1,64]{1,0:T(1,128)}, f32[1,64]{1,0:T(1,128)}) custom-call(bf16[512,256]{1,0:T(8,128)(2,1)} %get-tuple-element.19.r_0_, bf16[4,64,256]{2,1,0:T(8,128)(2,1)} %get-tuple-element.20.r_1_, ...), custom_call_target="tpu_custom_call" | custom-call | tf_op jit(solution)/shard_map/pallas_call | solution.py:669
